TPU v7x, 128 devices: a whole 4x4x4 slice. The times are simulated.
128 devices in a mesh: layer: 32 (over x, z, core), space: 4 (over y).
Axes of the slice: x: 4, y: 4, z: 4, core: 2. Of those that a mesh axis runs over, the one named last changes fastest.
Arguments:
- image_features: float32 [1, 64, 128, 128], P(None, None, 'space'), may hold values from -8 to 8
- output_cotangent: float32 [1, 64, 128, 128], P(None, None, 'space'), may hold values from -2.1 to 2.1
- conv_weights: bfloat16 [64, 9, 64, 64], P('layer'), may hold values from -0.25 to 0.25
Outputs:
- section_states: float32 [32, 1, 64, 128, 128], P('layer', None, None, 'space')
- start_adjoints: float32 [32, 1, 64, 128, 128], P('layer', None, None, 'space')
- weight_grads: float32 [64, 9, 64, 64], P('layer')
All inputs are finite; a program needn't handle non-finite values.
Results may differ from a plain program's by a relative error of at most 0.008.
Values may be sent and summed in bfloat16 or wider, within the bound.
A program may use at most 128 MiB of HBM per device.

v0:
```python
import jax
import jax.numpy as jnp
from jax import lax
from jax.sharding import PartitionSpec as P

ITERS = 2


horizon = 4.0
highest = lax.Precision.HIGHEST


def extended(block, sides, width):
    for axis, dim in sides:
        count = lax.axis_size(axis)
        forward = [(i, i + 1) for i in range(count - 1)]
        backward = [(target, source) for source, target in forward]
        low = lax.ppermute(
            lax.slice_in_dim(block, block.shape[dim] - width, None, axis=dim), axis, forward
        )
        high = lax.ppermute(lax.slice_in_dim(block, 0, width, axis=dim), axis, backward)
        block = jnp.concatenate([low, block, high], axis=dim)
    return block


def entering(part, axis, combine, identity, reverse):
    count = lax.axis_size(axis)
    place = lax.axis_index(axis)
    ahead = count - 1 - place if reverse else place
    gathered = jax.tree.map(lambda a: lax.all_gather(a, axis), part)
    state = jax.tree.map(lambda a, e: jnp.zeros_like(a) + jnp.asarray(e, a.dtype), part, identity)

    def one(lap, state):
        source = count - 1 - lap if reverse else lap
        return combine(
            state, jax.tree.map(lambda a: lax.dynamic_index_in_dim(a, source, 0, False), gathered)
        )

    return lax.fori_loop(0, ahead, one, state)


def pad_columns(values):
    return jnp.pad(values, ((0, 0), (0, 0), (0, 0), (1, 1)))


def stack_taps(padded, row_count, col_count, flipped):
    slices = []
    for tap_index in range(9):
        tap_row, tap_col = (tap_index // 3, tap_index % 3)
        if flipped:
            tap_row, tap_col = (2 - tap_row, 2 - tap_col)
        slices.append(padded[:, :, tap_row : tap_row + row_count, tap_col : tap_col + col_count])
    return jnp.concatenate(slices, axis=1)


def forward_conv(padded_rows, weight):
    row_count = padded_rows.shape[2] - 2
    col_count = padded_rows.shape[3]
    stacked = stack_taps(pad_columns(padded_rows), row_count, col_count, False)
    channels = weight.shape[1]
    flat_weight = jnp.transpose(weight, (1, 0, 2)).reshape(channels, 9 * channels)
    return jnp.einsum("ok,bkrw->borw", flat_weight, stacked, preferred_element_type=jnp.float32)


def backward_conv(padded_rows, weight):
    row_count = padded_rows.shape[2] - 2
    col_count = padded_rows.shape[3]
    stacked = stack_taps(pad_columns(padded_rows), row_count, col_count, True)
    channels = weight.shape[1]
    flat_weight = jnp.transpose(weight, (2, 0, 1)).reshape(channels, 9 * channels)
    return jnp.einsum("ck,bkrw->bcrw", flat_weight, stacked, preferred_element_type=jnp.float32)


def weight_grad(scaled, padded_rows):
    row_count = scaled.shape[2]
    col_count = scaled.shape[3]
    channels = scaled.shape[1]
    stacked = stack_taps(pad_columns(padded_rows), row_count, col_count, False)
    product = jnp.einsum("borw,bkrw->ok", scaled, stacked, preferred_element_type=jnp.float32)
    return jnp.transpose(product.reshape(channels, 9, channels), (1, 0, 2))


def mix_channels(matrix, field_state):
    return jnp.einsum("oc,bcrw->borw", matrix, field_state, precision=highest)


def compose(earlier, later):
    return (
        jnp.dot(later[0], earlier[0], precision=highest),
        mix_channels(later[0], earlier[1]) + later[1],
    )


def forward_sweep(field_state, weights, step_size, keep):
    layer_count = weights.shape[0]
    stored = []
    for layer_index in range(layer_count):
        rounded = extended(field_state.astype(jnp.bfloat16), (("space", 2),), 1)
        tangent = jnp.tanh(forward_conv(rounded, weights[layer_index]))
        field_state = field_state + step_size * tangent
        if keep:
            stored.append((rounded, tangent))
    return (field_state, stored)


def adjoint_sweep(adjoint, weights, stored, step_size, with_grads):
    layer_count = weights.shape[0]
    grad_list = [None] * layer_count
    for layer_index in reversed(range(layer_count)):
        rounded, tangent = stored[layer_index]
        scaled = (step_size * (1.0 - tangent * tangent) * adjoint).astype(jnp.bfloat16)
        rimmed = extended(scaled, (("space", 2),), 1)
        if with_grads:
            grad_list[layer_index] = weight_grad(scaled, rounded)
        adjoint = adjoint + backward_conv(rimmed, weights[layer_index])
    if with_grads:
        return (adjoint, jnp.stack(grad_list))
    return (adjoint, None)


def per_device(image_features, output_cotangent, conv_weights):
    layer_count = conv_weights.shape[0]
    step_size = horizon / (layer_count * lax.axis_size("layer"))
    channels = conv_weights.shape[2]
    summed = jnp.sum(conv_weights[0].astype(jnp.float32), axis=0)
    identity_matrix = jnp.eye(channels, dtype=jnp.float32)
    coarse = identity_matrix + layer_count * step_size * summed
    coarse_back = coarse.T
    field_state = image_features
    for iteration in range(ITERS):
        section_end, unused = forward_sweep(field_state, conv_weights, step_size, False)
        forward_residual = section_end - mix_channels(coarse, field_state)
        prefix_matrix, prefix_shift = entering(
            (coarse, forward_residual),
            "layer",
            compose,
            (identity_matrix, jnp.zeros_like(forward_residual)),
            False,
        )
        field_state = mix_channels(prefix_matrix, image_features) + prefix_shift
    final_end, stored = forward_sweep(field_state, conv_weights, step_size, True)
    adjoint_end = output_cotangent
    for iteration in range(ITERS):
        section_start, unused_grads = adjoint_sweep(
            adjoint_end, conv_weights, stored, step_size, False
        )
        residual = section_start - mix_channels(coarse_back, adjoint_end)
        suffix_matrix, suffix_shift = entering(
            (coarse_back, residual),
            "layer",
            compose,
            (identity_matrix, jnp.zeros_like(residual)),
            True,
        )
        adjoint_end = mix_channels(suffix_matrix, output_cotangent) + suffix_shift
    section_start, local_grads = adjoint_sweep(adjoint_end, conv_weights, stored, step_size, True)
    weight_grads = lax.psum(local_grads, "space")
    return (field_state[None], section_start[None], weight_grads)


def solution(mesh):
    placed = (
        P(None, None, "space", None),
        P(None, None, "space", None),
        P("layer", None, None, None),
    )
    return jax.shard_map(
        per_device,
        mesh=mesh,
        in_specs=placed,
        out_specs=(
            P("layer", None, None, "space", None),
            P("layer", None, None, "space", None),
            P("layer", None, None, None),
        ),
        check_vma=False,
    )
```

profile of v0, /device:TPU:0, one launch (start us, length us, event | category | flops | bytes accessed | tf_op | source)
XLA Modules:
  0.0 1156.6 jit_solution(3065451681628044214)
XLA Ops:
  9.2 3.6 collective-permute-start
  16.0 2.3 collective-permute-done.1
  22.6 3.5 collective-permute-start.2
  27.6 4.1 collective-permute-done.3
  38.2 28.0 %all_gather.38 = f32[32,64,64]{2,1,0:T(8,128)S(1)} all-gather(f32[1,64,64]{2,1,0:T(8,128)S(1)} %bitcast_add_fusion.2), channel_id=1, replica_groups=mesh['layer'=32,'space'=4] {'layer'}, dimensions={0}, use_global_device_ids=true | all-gather | bytes 540672 | tf_op jit(solution)/shard_map/all_gather | solution.py:30
  66.2 88.6 %all-gather.10.cloned.1.call-done = f32[32,64,32,128]{3,2,1,0:T(8,128)} async-done(((f32[1,64,32,128]{3,2,1,0:T(8,128)}), f32[32,64,32,128]{3,2,1,0:T(8,128)}) %all-gather.10.cloned.1.call-update) | async-done | bytes 33554448 | tf_op jit(solution)/shard_map/all_gather | solution.py:30
  156.6 3.4 collective-permute-start.4
  161.4 4.2 collective-permute-done.5
  168.8 3.4 collective-permute-start.6
  173.7 4.2 collective-permute-done.7
  183.8 206.6 %all-gather.12.cloned.1.call-done = f32[32,64,32,128]{3,2,1,0:T(8,128)} async-done(((f32[1,64,32,128]{3,2,1,0:T(8,128)}), f32[32,64,32,128]{3,2,1,0:T(8,128)}) %all-gather.12.cloned.1.call-update) | async-done | bytes 33554448 | tf_op jit(solution)/shard_map/all_gather | solution.py:30
  392.2 3.4 collective-permute-start.8
  397.0 4.2 collective-permute-done.9
  404.4 3.4 collective-permute-start.10
  409.3 4.1 collective-permute-done.11
  415.6 2.5 multiply_convert_fusion.2
  418.1 3.1 collective-permute-start.12
  422.6 4.2 collective-permute-done.13
  433.9 4.2 collective-permute-done.15
  444.6 121.8 %all-gather.2 = f32[2048,64]{1,0:T(8,128)} all-gather(f32[64,64]{1,0:T(8,128)S(1)} %copy.81), channel_id=4, replica_groups=mesh['layer'=32,'space'=4] {'layer'}, dimensions={0}, use_global_device_ids=true | all-gather | bytes 540672 | tf_op jit(solution)/shard_map/all_gather | solution.py:30
  566.4 85.3 %all-gather.14.cloned.1.call-done = f32[32,64,32,128]{3,2,1,0:T(8,128)} async-done(((f32[1,64,32,128]{3,2,1,0:T(8,128)}), f32[32,64,32,128]{3,2,1,0:T(8,128)}) %all-gather.14.cloned.1.call-update) | async-done | bytes 33554448 | tf_op jit(solution)/shard_map/all_gather | solution.py:30
  651.8 145.5 %while.54 = (s32[]{:T(128)}, f32[64,64]{1,0:T(8,128)S(1)}, f32[1,64,32,128]{3,1,2,0:T(8,128)S(1)}, s32[]{:T(128)}, f32[32,64,64]{2,1,0:T(8,128)}, /*index=5*/f32...) while((s32[]{:T(128)}, f32[64,64]{1,0:T(8,128)S(1)}, ...), condition=%wide.region_6.7_spmd, body=%wide.region_5.6_spmd.sunk | while | flops 204734464 | bytes 7471263 | solution.py:39
  653.2 2.3 fusion.301
  676.6 2.3 fusion.301
  700.1 2.3 fusion.301
  709.5 2.3 fusion.301
  718.9 2.3 fusion.301
  747.0 2.3 fusion.301
  779.9 2.3 fusion.301
  789.3 2.3 fusion.301
  797.2 2.9 multiply_convert_fusion.1
  800.1 3.3 collective-permute-start.16
  804.9 4.2 collective-permute-done.17
  812.3 3.4 collective-permute-start.18
  817.2 4.2 collective-permute-done.19
  828.8 106.9 %all-gather.16.cloned.1.call-done = f32[32,64,32,128]{3,2,1,0:T(8,128)} async-done(((f32[1,64,32,128]{3,2,1,0:T(8,128)}), f32[32,64,32,128]{3,2,1,0:T(8,128)}) %all-gather.16.cloned.1.call-update) | async-done | bytes 33554448 | tf_op jit(solution)/shard_map/all_gather | solution.py:30
  935.9 145.3 %while.55 = (s32[]{:T(128)}, f32[64,64]{1,0:T(8,128)S(1)}, f32[1,64,32,128]{3,1,2,0:T(8,128)S(1)}, s32[]{:T(128)}, f32[32,64,64]{2,1,0:T(8,128)}, /*index=5*/f32...) while((s32[]{:T(128)}, f32[64,64]{1,0:T(8,128)S(1)}, ...), condition=%wide.region_8.9_spmd, body=%wide.region_7.8_spmd.sunk | while | flops 204734464 | bytes 7471263 | solution.py:39
  998.3 2.3 fusion.307
  1012.3 2.3 fusion.307
  1026.4 2.3 fusion.307
  1054.5 2.3 fusion.307
  1068.6 2.3 fusion.307
  1081.2 2.9 multiply_convert_fusion
  1084.1 3.5 collective-permute-start.20
  1089.1 4.6 convolution_bitcast_fusion.12
  1100.2 4.6 collective-permute-start.22
  1106.9 3.4 collective-permute-done.23
  1115.1 32.8 %all-reduce.14.cloned.1.call-done = f32[2,9,64,64]{3,2,1,0:T(8,128)} async-done(((f32[2,9,64,64]{3,2,1,0:T(8,128)}), f32[2,9,64,64]{3,2,1,0:T(8,128)}) %all-reduce.14.cloned.1.call-update) | async-done | bytes 294928 | tf_op jit(solution)/shard_map/psum | solution.py:157
  (536 shorter events, 342.6 us)
Async XLA Ops:
  7.2 12.4 %copy-start = (f32[1,64,32,128]{3,2,1,0:T(8,128)S(1)}, f32[1,64,32,128]{3,2,1,0:T(8,128)}, u32[]{:S(2)}) copy-start(f32[1,64,32,128]{3,2,1,0:T(8,128)} %param.11) | copy-start | bytes 3145732
  7.2 147.6 %all-gather.10.cloned.1.call-start = ((), (), s32[]{:S(2)}) async-start(), calls=%async_computation.1 | async-start | bytes 34603008 | tf_op jit(solution)/shard_map/all_gather | solution.py:30
  9.2 6.9 collective-permute-start
  12.7 5.6 collective-permute-start.1
  16.0 5.0 copy-start.7
  20.6 6.8 copy-start.10
  22.6 5.0 collective-permute-start.2
  26.1 5.6 collective-permute-start.3
  38.1 352.3 %all-gather.12.cloned.1.call-start = ((), (), s32[]{:S(2)}) async-start(), calls=%async_computation.2 | async-start | bytes 34603008 | tf_op jit(solution)/shard_map/all_gather | solution.py:30
  156.6 4.8 collective-permute-start.4
  160.0 5.6 collective-permute-start.5
  166.2 1.6 copy-start.8
  168.8 4.9 collective-permute-start.6
  172.2 5.6 collective-permute-start.7
  183.7 467.9 %all-gather.14.cloned.1.call-start = ((), (), s32[]{:S(2)}) async-start(), calls=%async_computation.3 | async-start | bytes 34603008 | tf_op jit(solution)/shard_map/all_gather | solution.py:30
  392.1 11.2 copy-start.4
  392.2 4.8 collective-permute-start.8
  395.6 5.6 collective-permute-start.9
  401.8 1.6 copy-start.9
  403.3 10.8 copy-start.2
  404.4 4.9 collective-permute-start.10
  407.8 5.6 collective-permute-start.11
  414.0 1.5 copy-start.1
  415.5 12.1 %copy-start.3 = (bf16[1,576,32,128]{3,1,2,0:T(8,128)(2,1)}, bf16[1,576,32,128]{3,1,2,0:T(8,128)(2,1)S(1)}, u32[]{:S(2)}) copy-start(bf16[1,576,32,128]{3,1,2,0:T(8,128)(2,1)S(1)} %slice_dynamic-update-slice_fusion.36) | copy-start | bytes 14155780
  418.1 4.5 collective-permute-start.12
  421.2 5.6 collective-permute-start.13
  427.4 1.5 copy-start.6
  430.5 3.4 collective-permute-start.14
  432.4 5.6 collective-permute-start.15
  444.4 491.3 %all-gather.16.cloned.1.call-start = ((), (), s32[]{:S(2)}) async-start(), calls=%async_computation.4 | async-start | bytes 34603008 | tf_op jit(solution)/shard_map/all_gather | solution.py:30
  800.1 4.8 collective-permute-start.16
  803.5 5.6 collective-permute-start.17
  812.3 4.9 collective-permute-start.18
  815.7 5.6 collective-permute-start.19
  824.5 2.8 copy-start.5
  827.2 320.7 %all-reduce.14.cloned.1.call-start = ((), (), s32[]{:S(2)}) async-start(), calls=%async_computation | async-start | bytes 1179648 | tf_op jit(solution)/shard_map/psum | solution.py:157
  1084.1 9.6 collective-permute-start.20
  1087.6 6.1 collective-permute-start.21
  1095.6 2.2 slice-start
  1095.8 2.2 slice-start.1
  1100.2 6.7 collective-permute-start.22
  1104.7 5.6 collective-permute-start.23
Sparse Core Ops, SparseCore 0:
  38.2 116.5 all-gather.9
  183.9 206.4 all-gather.11
  444.5 207.0 all-gather.13
  827.3 108.4 all-gather.15
  1107.1 40.7 all-reduce.13
where the time goes:
time: 1180 us; the launch traced here: 1160 us
  waiting for transfers between devices  564 us (48%)
  matrix products  237 us (20%)
  blocking collectives  150 us (13%)
  local copies, waits for them, and re-layouts  120 us (10%)
  starting transfers between devices  56.9 us (5%)
  between operations  15.7 us (1%)
    all_gather x4, waiting for transfers between devices, entering(): gathered = jax.tree.map(lambda a: lax.all_gather(a, axis), part)  487 us
    dot_general x70, matrix products, mix_channels(): return jnp.einsum('oc,bcrw->borw', matrix, field_state, precision=highest)  157 us
    all_gather x2, blocking collectives, entering(): gathered = jax.tree.map(lambda a: lax.all_gather(a, axis), part)  150 us
    dynamic_slice x62, local copies, waits for them, and re-layouts, one(): lax.dynamic_index_in_dim(a, source, 0, False)  80.5 us
    dot_general x62, matrix products, compose(): jnp.dot(later[0], earlier[0], precision=highest)  57.3 us
    ppermute x12, waiting for transfers between devices, extended(): lax.ppermute(lax.slice_in_dim(block, 0, width, axis=dim), axis, backward)  43.3 us
    ppermute x12, starting transfers between devices, extended(): lax.ppermute(lax.slice_in_dim(block, block.shape[dim] - width, None, axis...  40.4 us
    psum x1, waiting for transfers between devices, per_device(): weight_grads = lax.psum(local_grads, 'space')  32.8 us
  transfers between devices with their start and end apart: 29, of which 21 were waited for; matrix products, arithmetic and copies ran while one was open for 1% of the time, Pallas kernels for 0%

commit v1 on v0

v1 whole, which is shorter than its diff:
```python
import functools

import jax
import jax.numpy as jnp
from jax import lax
from jax.experimental import pallas as pl
from jax.experimental.pallas import tpu as pltpu
from jax.sharding import PartitionSpec as P

ITERS = 2
HORIZON = 4.0
HALO = 4
MESH = pl.DeviceIdType.MESH
F32 = jnp.float32
BF16 = jnp.bfloat16


def kernel(
    nl, ns, rows, ch, cols, step_size,
    u_in, c_in, wf, wb, bb, bbt,
    states_out, adj_out, grads_out,
    u, s, c, a, a1, t0, t1, y0, y1, x0, x1, d0, d1,
    sendq, recvq, sendx, recvx, mb, mbt, grad, grecv, gsum,
    in_sem, out_sem, uh_send, uh_recv, ch_send, ch_recv,
    b_send, b_recv, bt_send, bt_recv, q_send, q_recv, x_send, x_recv, h_send, h_recv,
    g_send, g_recv, r_send, r_recv,
):
    me = lax.axis_index("layer")
    space = lax.axis_index("space")
    ext = rows + 2 * HALO
    pairs = ext // 2
    quarter = grad.shape[0] // ns
    has_up = space > 0
    has_down = space < ns - 1

    def loop(lo, hi, body):
        def step(i, carry):
            body(i)
            return carry
        lax.fori_loop(lo, hi, step, 0)

    def partner(i):
        return lax.rem(me + i, nl)

    def neighbour(i):
        return lax.rem(space + i, ns)

    in_u = pltpu.make_async_copy(u_in, u.at[pl.ds(HALO, rows)], in_sem.at[0])
    in_c = pltpu.make_async_copy(c_in, c.at[pl.ds(HALO, rows)], in_sem.at[1])
    in_u.start()
    in_c.start()

    blank = jnp.zeros((HALO, ch, cols), F32)
    for ref in (u, c):
        ref[pl.ds(0, HALO)] = blank
        ref[pl.ds(HALO + rows, HALO)] = blank
    blank16 = jnp.zeros((HALO, ch, cols), BF16)
    for ph in range(2 * ITERS):
        recvx[ph, pl.ds(0, HALO)] = blank16
        recvx[ph, pl.ds(HALO + rows, HALO)] = blank16
    for ref in (d0, d1):
        ref[pl.ds(0, HALO)] = blank16
        ref[pl.ds(HALO + rows, HALO)] = blank16
    for ref in (y0, y1):
        for e in (0, 1, 2, ext - 1, ext, ext + 1):
            ref[e] = jnp.zeros((3 * ch, cols), F32)

    barrier = pltpu.get_barrier_semaphore()

    def greet(i):
        pl.semaphore_signal(barrier, inc=1, device_id={"layer": partner(i)}, device_id_type=MESH)
    loop(1, nl, greet)

    def greet_space(i):
        pl.semaphore_signal(barrier, inc=1, device_id={"space": neighbour(i)}, device_id_type=MESH)
    loop(1, ns, greet_space)

    pl.semaphore_wait(barrier, nl - 1 + ns - 1)

    mb[me] = bb[...]
    mbt[me] = bbt[...]

    def b_copy(i, src, dst, send, recv):
        k = partner(i)
        return pltpu.make_async_remote_copy(
            src_ref=src, dst_ref=dst.at[me], send_sem=send.at[k], recv_sem=recv.at[me],
            device_id={"layer": k}, device_id_type=MESH)

    def send_b(i):
        b_copy(i, bb, mb, b_send, b_recv).start()
    loop(1, nl, send_b)

    def halo_copies(src, dst, width, send, recv, axis_space):
        up = pltpu.make_async_remote_copy(
            src_ref=src.at[pl.ds(HALO, width)], dst_ref=dst.at[pl.ds(HALO + rows, width)],
            send_sem=send.at[0], recv_sem=recv.at[1],
            device_id={"space": lax.rem(space + ns - 1, ns)}, device_id_type=MESH)
        down = pltpu.make_async_remote_copy(
            src_ref=src.at[pl.ds(HALO + rows - width, width)],
            dst_ref=dst.at[pl.ds(HALO - width, width)],
            send_sem=send.at[1], recv_sem=recv.at[0],
            device_id={"space": lax.rem(space + 1, ns)}, device_id_type=MESH)
        return up, down

    def halo_start(copies):
        up, down = copies

        @pl.when(has_up)
        def _():
            up.start()

        @pl.when(has_down)
        def _():
            down.start()

    def halo_wait(copies):
        up, down = copies

        @pl.when(has_up)
        def _():
            up.wait_send()
            down.wait_recv()

        @pl.when(has_down)
        def _():
            down.wait_send()
            up.wait_recv()

    in_u.wait()
    u_halo = halo_copies(u, u, HALO, uh_send, uh_recv, space)
    halo_start(u_halo)
    in_c.wait()
    c_halo = halo_copies(c, c, 2, ch_send, ch_recv, space)
    halo_start(c_halo)

    def send_bt(i):
        b_copy(i, bbt, mbt, bt_send, bt_recv).start()
    loop(1, nl, send_bt)

    halo_wait(u_halo)

    lane = lax.broadcasted_iota(jnp.int32, (ch, cols), 1)
    not_first = lane > 0
    not_last = lane < cols - 1

    def shifted(v):
        left = jnp.where(not_first, pltpu.roll(v, 1, 1), 0.0)
        right = jnp.where(not_last, pltpu.roll(v, cols - 1, 1), 0.0)
        return jnp.concatenate([left.astype(BF16), v.astype(BF16), right.astype(BF16)], axis=0)

    def inside(e):
        return jnp.logical_and(
            jnp.logical_or(e >= HALO, has_up), jnp.logical_or(e < HALO + rows, has_down))

    def convolve(p, low, high, weight, y, keep):
        pair = jnp.concatenate([shifted(low), shifted(high)], axis=1)
        if keep is not None:
            keep[p] = pair
        out = jnp.dot(weight, pair, preferred_element_type=F32)
        y[2 * p + 1] = out[:, :cols]
        y[2 * p + 2] = out[:, cols:]

    def gathered(y, e):
        return y[e, 0:ch] + y[e + 1, ch:2 * ch] + y[e + 2, 2 * ch:3 * ch]

    def forward_sweep(state, lo, hi, keep, finish):
        def first(p):
            convolve(p, state[2 * p], state[2 * p + 1], wf[0], y0, x0 if keep else None)
        loop(lo, hi, first)

        def second(p):
            out = []
            for e in (2 * p, 2 * p + 1):
                tangent = jnp.tanh(gathered(y0, e))
                t0[e] = tangent
                out.append(jnp.where(inside(e), state[e] + step_size * tangent, 0.0))
            convolve(p, out[0], out[1], wf[1], y1, x1 if keep else None)
        loop(lo, hi, second)
        finish()

    def start_q(ph, r):
        pltpu.make_async_remote_copy(
            src_ref=sendq.at[ph, r], dst_ref=recvq.at[ph, me],
            send_sem=q_send.at[r], recv_sem=q_recv.at[ph, me],
            device_id={"layer": r}, device_id_type=MESH).start()

    def give_q(ph, i, r, value):
        if ph % ITERS:
            value = value - sendq[ph - 1, r].astype(F32)
        rounded = value.astype(BF16)
        sendq[ph, r] = rounded

        @pl.when(i == 0)
        def _():
            recvq[ph, r] = rounded

        @pl.when(i > 0)
        def _():
            start_q(ph, r)

    def wait_q(ph):
        def one(i):
            k = partner(i)
            copy = pltpu.make_async_remote_copy(
                src_ref=sendq.at[ph, k], dst_ref=recvq.at[ph, k],
                send_sem=q_send.at[k], recv_sem=q_recv.at[ph, k],
                device_id={"layer": k}, device_id_type=MESH)
            copy.wait_send()
            copy.wait_recv()
        loop(1, nl, one)

    def scan(ph, matrices, reverse):
        def place(i):
            return nl - 1 - i if reverse else i

        def one(i, state):
            j, following = place(i), place(i + 1)
            shift = recvq[ph, j].astype(F32)
            sendx[ph, j] = state.astype(BF16)
            if ph % ITERS:
                shift = (shift + recvq[ph - 1, j].astype(F32)
                         + sendx[ph - 1, j].astype(F32) - sendx[ph - 1, following].astype(F32))
            high = state.astype(BF16)
            low = (state - high.astype(F32)).astype(BF16)
            matrix = matrices[j]
            mixed = jnp.dot(
                jnp.concatenate([matrix, matrix], axis=1),
                jnp.concatenate([high, high, low, low], axis=0), preferred_element_type=F32)
            return state + mixed + shift
        state = lax.fori_loop(0, nl - 1, one, jnp.zeros((ch, cols), F32))
        sendx[ph, place(nl - 1)] = state.astype(BF16)

        recvx[ph, HALO + me] = sendx[ph, me]

        def give(i):
            x_copy(ph, partner(i), me).start()
        loop(1, nl, give)

    def x_copy(ph, k, row):
        return pltpu.make_async_remote_copy(
            src_ref=sendx.at[ph, k], dst_ref=recvx.at[ph, HALO + row],
            send_sem=x_send.at[k], recv_sem=x_recv.at[ph, row],
            device_id={"layer": k}, device_id_type=MESH)

    def wait_x(ph, width):
        def take(k):
            @pl.when(k != me)
            def _():
                x_copy(ph, k, k).wait_recv()
        loop(0, HALO, take)
        loop(rows - HALO, rows, take)
        copies = halo_copies(recvx.at[ph], recvx.at[ph], width, h_send.at[ph], h_recv.at[ph], space)
        halo_start(copies)
        loop(HALO, rows - HALO, take)

        def sent(i):
            k = partner(i)
            x_copy(ph, k, k).wait_send()
        loop(1, nl, sent)
        halo_wait(copies)

    for iteration in range(ITERS):
        ph = iteration

        def finish(ph=ph):
            def one(i):
                r = partner(i)
                e = r + HALO
                tangent = jnp.tanh(gathered(y1, e))
                give_q(ph, i, r, step_size * (t0[e] + tangent))
            loop(0, nl, one)
        forward_sweep(u if iteration == 0 else s, 1, pairs - 1, False, finish)
        wait_q(ph)
        if iteration == 0:
            def settle_b(i):
                k = partner(i)
                for src, dst, send, recv in ((bb, mb, b_send, b_recv), (bbt, mbt, bt_send, bt_recv)):
                    copy = pltpu.make_async_remote_copy(
                        src_ref=src, dst_ref=dst.at[k], send_sem=send.at[k], recv_sem=recv.at[k],
                        device_id={"layer": k}, device_id_type=MESH)
                    copy.wait_send()
                    copy.wait_recv()
            loop(1, nl, settle_b)
        scan(ph, mb, False)
        wait_x(ph, HALO)
        before = u if iteration == 0 else s

        def update(e, ph=ph, before=before):
            s[e] = before[e] + recvx[ph, e].astype(F32)
        loop(0, ext, update)

    states = pltpu.make_async_copy(s.at[pl.ds(HALO, rows)], states_out, out_sem.at[0])
    states.start()
    halo_wait(c_halo)

    def finish_last():
        def one(p):
            for e in (2 * p, 2 * p + 1):
                t1[e] = jnp.tanh(gathered(y1, e))
        loop(1, pairs - 1, one)
    forward_sweep(s, 0, pairs, True, finish_last)

    def adjoint_sweep(state, keep, finish):
        def scaled(tangent, value):
            return step_size * (1.0 - tangent * tangent) * value

        def first(p):
            out = []
            for e in (2 * p, 2 * p + 1):
                value = scaled(t1[e], state[e])
                if keep:
                    d1[e] = value.astype(BF16)
                out.append(value)
            convolve(p, out[0], out[1], wb[1], y0, None)
        loop(1, pairs - 1, first)

        def second(p):
            out = []
            for e in (2 * p, 2 * p + 1):
                after = state[e] + gathered(y0, e)
                a1[e] = after
                value = jnp.where(inside(e), scaled(t0[e], after), 0.0)
                if keep:
                    d0[e] = value.astype(BF16)
                out.append(value)
            convolve(p, out[0], out[1], wb[0], y1, None)
        loop(1, pairs - 1, second)
        finish()

    for iteration in range(ITERS):
        ph = ITERS + iteration

        def finish_adjoint(ph=ph):
            def one(i):
                r = partner(i)
                e = r + HALO
                give_q(ph, i, r, gathered(y0, e) + gathered(y1, e))
            loop(0, nl, one)
        before = c if iteration == 0 else a
        adjoint_sweep(before, False, finish_adjoint)
        wait_q(ph)
        scan(ph, mbt, True)
        wait_x(ph, 2)

        def update_adjoint(e, ph=ph, before=before):
            a[e] = before[e] + recvx[ph, e].astype(F32)
        loop(0, ext, update_adjoint)

    def finish_start():
        def one(e):
            a1[e] = a1[e] + gathered(y1, e)
        loop(HALO, HALO + rows, one)
    adjoint_sweep(a, True, finish_start)
    starts = pltpu.make_async_copy(a1.at[pl.ds(HALO, rows)], adj_out, out_sem.at[1])
    starts.start()

    for ref in (d0, d1):
        ref[pl.ds(0, HALO)] = blank16
        ref[pl.ds(HALO + rows, HALO)] = blank16
    for index, (d, x) in enumerate(((d0, x0), (d1, x1))):
        part = pl.ds(index * 3 * ch, 3 * ch)
        grad[part] = jnp.zeros((3 * ch, 3 * ch), F32)

        def add(p, d=d, x=x, part=part):
            e = 2 * p
            left = jnp.concatenate([d[e + 1], d[e], d[e - 1]], axis=0)
            right = jnp.concatenate([d[e + 2], d[e + 1], d[e]], axis=0)
            grad[part] += lax.dot_general(
                jnp.concatenate([left, right], axis=1), x[p], (((1,), (1,)), ((), ())),
                preferred_element_type=F32)
        loop(1, pairs - 1, add)

    def g_copy(i):
        k = neighbour(i)
        return pltpu.make_async_remote_copy(
            src_ref=grad.at[pl.ds(k * quarter, quarter)], dst_ref=grecv.at[space],
            send_sem=g_send.at[k], recv_sem=g_recv.at[space],
            device_id={"space": k}, device_id_type=MESH)

    def g_arrival(i):
        k = neighbour(i)
        return pltpu.make_async_remote_copy(
            src_ref=grad.at[pl.ds(k * quarter, quarter)], dst_ref=grecv.at[k],
            send_sem=g_send.at[k], recv_sem=g_recv.at[k],
            device_id={"space": k}, device_id_type=MESH)

    for i in range(1, ns):
        g_copy(i).start()
    total = grad[pl.ds(pl.multiple_of(space * quarter, quarter), quarter)]
    for i in range(1, ns):
        g_arrival(i).wait_recv()
        total = total + grecv[neighbour(i)]
    own = pl.ds(pl.multiple_of(space * quarter, quarter), quarter)
    gsum[own] = total

    def r_copy(i, source):
        k = neighbour(i)
        part = pl.ds(source * quarter, quarter)
        return pltpu.make_async_remote_copy(
            src_ref=gsum.at[part], dst_ref=gsum.at[part],
            send_sem=r_send.at[k], recv_sem=r_recv.at[source],
            device_id={"space": k}, device_id_type=MESH)

    for i in range(1, ns):
        r_copy(i, space).start()
    for i in range(1, ns):
        g_arrival(i).wait_send()
        r_copy(i, neighbour(i)).wait_recv()
        r_copy(i, space).wait_send()
    grads = pltpu.make_async_copy(gsum, grads_out, out_sem.at[2])
    grads.start()
    states.wait()
    starts.wait()
    grads.wait()


def split(matrix):
    high = matrix.astype(BF16)
    low = (matrix - high.astype(F32)).astype(BF16)
    return jnp.concatenate([high, low], axis=1)


def per_device(image_features, output_cotangent, conv_weights):
    nl, ns = lax.axis_size("layer"), lax.axis_size("space")
    layers, _, ch, _ = conv_weights.shape
    _, _, rows, cols = image_features.shape
    assert rows == nl and layers == 2 and cols == 2 * ch
    step_size = HORIZON / (layers * nl)
    ext = rows + 2 * HALO

    taps = conv_weights.reshape(layers, 3, 3, ch, ch)
    wf = taps.transpose(0, 1, 3, 2, 4).reshape(layers, 3 * ch, 3 * ch)
    wb = taps[:, ::-1, ::-1].transpose(0, 1, 4, 2, 3).reshape(layers, 3 * ch, 3 * ch)
    coarse = layers * step_size * jnp.sum(conv_weights[0].astype(F32), axis=0)

    u_in = image_features[0].transpose(1, 0, 2)
    c_in = output_cotangent[0].transpose(1, 0, 2)

    field = functools.partial(pltpu.VMEM, (ext, ch, cols))
    any_spec = pl.BlockSpec(memory_space=pl.ANY)
    vmem_spec = pl.BlockSpec(memory_space=pltpu.VMEM)
    dma = pltpu.SemaphoreType.DMA
    phases = 2 * ITERS
    states, starts, grads = pl.pallas_call(
        functools.partial(kernel, nl, ns, rows, ch, cols, step_size),
        out_shape=(
            jax.ShapeDtypeStruct((rows, ch, cols), F32),
            jax.ShapeDtypeStruct((rows, ch, cols), F32),
            jax.ShapeDtypeStruct((layers * 3 * ch, 3 * ch), F32),
        ),
        in_specs=[any_spec, any_spec, vmem_spec, vmem_spec, vmem_spec, vmem_spec],
        out_specs=(any_spec, any_spec, any_spec),
        scratch_shapes=[
            field(F32), field(F32), field(F32), field(F32), field(F32), field(F32), field(F32),
            pltpu.VMEM((ext + 2, 3 * ch, cols), F32),
            pltpu.VMEM((ext + 2, 3 * ch, cols), F32),
            pltpu.VMEM((ext // 2, 3 * ch, 2 * cols), BF16),
            pltpu.VMEM((ext // 2, 3 * ch, 2 * cols), BF16),
            field(BF16), field(BF16),
            pltpu.VMEM((phases, rows, ch, cols), BF16),
            pltpu.VMEM((phases, nl, ch, cols), BF16),
            pltpu.VMEM((phases, nl, ch, cols), BF16),
            pltpu.VMEM((phases, ext, ch, cols), BF16),
            pltpu.VMEM((nl, ch, 2 * ch), BF16),
            pltpu.VMEM((nl, ch, 2 * ch), BF16),
            pltpu.VMEM((layers * 3 * ch, 3 * ch), F32),
            pltpu.VMEM((ns, layers * 3 * ch // ns, 3 * ch), F32),
            pltpu.VMEM((layers * 3 * ch, 3 * ch), F32),
            dma((2,)), dma((3,)), dma((2,)), dma((2,)), dma((2,)), dma((2,)),
            dma((nl,)), dma((nl,)), dma((nl,)), dma((nl,)),
            dma((nl,)), dma((phases, nl)), dma((nl,)), dma((phases, nl)),
            dma((phases, 2)), dma((phases, 2)),
            dma((ns,)), dma((ns,)), dma((ns,)), dma((ns,)),
        ],
        compiler_params=pltpu.CompilerParams(
            collective_id=0, has_side_effects=True, vmem_limit_bytes=56 * 1024 * 1024),
        name="mgrit",
    )(u_in, c_in, wf, wb, split(coarse), split(coarse.T))

    grads = grads.reshape(layers, 3, ch, 3, ch).transpose(0, 1, 3, 2, 4)
    return (
        states.transpose(1, 0, 2)[None, None],
        starts.transpose(1, 0, 2)[None, None],
        grads.reshape(layers, 9, ch, ch),
    )


def solution(mesh):
    placed = (
        P(None, None, "space", None),
        P(None, None, "space", None),
        P("layer", None, None, None),
    )
    return jax.shard_map(
        per_device,
        mesh=mesh,
        in_specs=placed,
        out_specs=(
            P("layer", None, None, "space", None),
            P("layer", None, None, "space", None),
            P("layer", None, None, None),
        ),
        check_vma=False,
    )
```

time: 1180 us -> 211 us (0.18); the launches traced: 1160 us -> 211 us
  waiting for transfers between devices: 564 us -> 0 us
  matrix products: 237 us -> 0 us
  Pallas kernels: 0 us -> 196 us
  blocking collectives: 150 us -> 0 us
  local copies, waits for them, and re-layouts: 120 us -> 13.3 us
  starting transfers between devices: 56.9 us -> 0 us
  between operations: 15.7 us -> 0.73 us
    all_gather x4 -> x0, waiting for transfers between devices: 487 us -> none  [entering(): gathered = jax.tree.map(lambda a: lax.all_gather(a, axis), part)]
    dot_general x146 -> x0, matrix products: 237 us -> none  [the longest x70 157 us: mix_channels(): return jnp.einsum('oc,bcrw->borw', matrix, field_state, precision=highest)]
    pallas_call x0 -> x1, Pallas kernels: none -> 196 us  [per_device(): pl.pallas_call(functools.partial(kernel, nl, ns, rows, ch, cols, step_siz...]
    all_gather x2 -> x0, blocking collectives: 150 us -> none  [entering(): gathered = jax.tree.map(lambda a: lax.all_gather(a, axis), part)]
    dynamic_slice x62 -> x0, local copies, waits for them, and re-layouts: 80.5 us -> none  [one(): lax.dynamic_index_in_dim(a, source, 0, False)]
    ppermute x24 -> x0, starting transfers between devices: 56.7 us -> none  [the longest x12 40.4 us: extended(): lax.ppermute(lax.slice_in_dim(block, block.shape[dim] - width, None, axis...]
    ppermute x24 -> x0, waiting for transfers between devices: 44 us -> none  [the longest x12 43.3 us: extended(): lax.ppermute(lax.slice_in_dim(block, 0, width, axis=dim), axis, backward)]
    psum x1 -> x0, waiting for transfers between devices: 32.8 us -> none  [per_device(): weight_grads = lax.psum(local_grads, 'space')]
  transfers between devices with their start and end apart: 29 -> 0, of which waited for: 21 -> 0; matrix products, arithmetic and copies ran while one was open for 1% -> 0% of each run, Pallas kernels for 0% -> 0%
where the time goes in v1:
time: 211 us
  Pallas kernels  196 us (93%)
  local copies, waits for them, and re-layouts  13.3 us (6%)
    pallas_call x1, Pallas kernels, per_device(): pl.pallas_call(functools.partial(kernel, nl, ns, rows, ch, cols, step_siz...  196 us
    unnamed x12, local copies, waits for them, and re-layouts  4.5 us

profile of v1, /device:TPU:0, one launch (start us, length us, event | category | flops | bytes accessed | tf_op | source)
XLA Modules:
  0.0 211.3 jit_solution(2698707104660557322)
XLA Ops:
  0.6 0.0 copy-start
  0.6 1.0 convert_reduce_fusion
  1.7 0.1 copy.35
  1.8 0.7 pad_maximum_fusion.1.bbt
  2.5 0.7 copy.36.bb
  3.1 0.0 copy-done
  3.2 0.2 copy.34
  3.4 0.0 copy-start.3
  3.4 1.5 rev.3
  4.9 0.0 copy-start.2
  4.9 0.9 reshape.24.wb
  5.8 0.3 copy.44
  6.1 0.9 reshape.23.wf
  7.0 0.0 copy-done.3
  7.0 0.0 copy-done.2
  7.0 2.5 %copy_bitcast_fusion = (f32[32,64,128]{2,1,0:T(8,128)}, f32[32,64,128]{2,1,0:T(8,128)}) fusion(f32[1,64,32,128]{3,2,1,0:T(8,128)S(1)} %copy-done.2, f32[1,64,32,128]{3,2,1,0:T(8,128)S(1)} %copy-done.3), kind=kLoop, calls=%fused_computation | loop fusion | bytes 4194304 | tf_op jit(solution)/shard_map/transpose | solution.py:437
  9.6 195.5 %mgrit.1 = (f32[32,64,128]{2,1,0:T(8,128)}, f32[32,64,128]{2,1,0:T(8,128)}, f32[384,192]{1,0:T(8,128)}) custom-call(f32[32,64,128]{2,1,0:T(8,128)} %get-tuple-element.25.u_in, f32[32,64,128]{2,1,0:T(8,128)} %get-tuple-element.24.c_in, bf16[2,192,192]{2,1,0:T(8,128)(2,1)} %reshape.23.wf, bf16[2,192,192]{2,1,0:T(8,128)(2,1)} %reshape.24.wb, ...), custom_call_target="tpu_custom_call" | custom-call | tf_op jit(solution)/shard_map/mgrit/pallas_call | solution.py:444
  205.1 0.0 copy-start.1
  205.1 2.9 %copy.39 = f32[1,1,64,32,128]{4,3,2,1,0:T(8,128)} copy(f32[1,1,64,32,128]{4,2,3,1,0:T(8,128)} %bitcast.36) | data formatting | bytes 2097152
  208.0 0.0 copy-done.1
  208.0 0.0 copy-start.4
  208.0 1.6 copy.40
  209.6 0.0 copy-done.4
  209.6 0.1 copy.37
  209.7 0.4 reshape.25
  210.1 1.1 copy.38
  (3 shorter events, 0.0 us)
Async XLA Ops:
  0.6 2.5 %copy-start = (bf16[2,9,64,64]{3,2,1,0:T(8,128)(2,1)S(1)}, bf16[2,9,64,64]{3,2,1,0:T(8,128)(2,1)}, u32[]{:S(2)}) copy-start(bf16[2,9,64,64]{3,2,1,0:T(8,128)(2,1)} %param.5) | copy-start | bytes 442372
  3.4 3.6 %copy-start.3 = (f32[1,64,32,128]{3,2,1,0:T(8,128)S(1)}, f32[1,64,32,128]{3,2,1,0:T(8,128)}, u32[]{:S(2)}) copy-start(f32[1,64,32,128]{3,2,1,0:T(8,128)} %param.3) | copy-start | bytes 3145732
  4.9 2.1 %copy-start.2 = (f32[1,64,32,128]{3,2,1,0:T(8,128)S(1)}, f32[1,64,32,128]{3,2,1,0:T(8,128)}, u32[]{:S(2)}) copy-start(f32[1,64,32,128]{3,2,1,0:T(8,128)} %param.4) | copy-start | bytes 3145732
  205.1 2.9 %copy-start.1 = (f32[32,64,128]{2,1,0:T(8,128)S(1)}, f32[32,64,128]{2,1,0:T(8,128)}, u32[]{:S(2)}) copy-start(f32[32,64,128]{2,1,0:T(8,128)} %get-tuple-element.7) | copy-start | bytes 3145732
  208.0 1.6 copy-start.4

commit v2 on v0

v2 whole, which is shorter than its diff:
```python
import functools

import jax
import jax.numpy as jnp
from jax import lax
from jax.experimental import pallas as pl
from jax.experimental.pallas import tpu as pltpu
from jax.sharding import PartitionSpec as P

ITERS = 2
HORIZON = 4.0
HALO = 4
GROUP = 4
MESH = pl.DeviceIdType.MESH
F32 = jnp.float32
BF16 = jnp.bfloat16


def kernel(
    nl, ns, rows, ch, cols, step_size,
    u_in, c_in, w_in,
    states_out, adj_out, grads_out,
    u, s, c, a, a1, t0, t1, y0, y1, x0, x1, d0, d1,
    sendq, recvq, sendx, recvx, w, wf, wb, mb, rev_m, fwd_p, rev_p, ys,
    grad, grecv, gsum, gout,
    in_sem, out_sem, uh_send, uh_recv, ch_send, ch_recv,
    b_send, b_recv, q_send, q_recv, x_send, x_recv, h_send, h_recv,
    g_send, g_recv, r_send, r_recv,
):
    me = lax.axis_index("layer")
    space = lax.axis_index("space")
    ext = rows + 2 * HALO
    pairs = ext // 2
    own = rows // 2
    groups = nl // GROUP
    has_up = space > 0
    has_down = space < ns - 1

    def loop(lo, hi, body):
        def step(i, carry):
            body(i)
            return carry
        lax.fori_loop(lo, hi, step, 0)

    def partner(i):
        return lax.rem(me + i, nl)

    def neighbour(i):
        return lax.rem(space + i, ns)

    in_w = pltpu.make_async_copy(w_in, w, in_sem.at[2])
    in_w.start()
    for r in range(rows):
        pltpu.make_async_copy(u_in.at[:, r, 0], u.at[HALO + r], in_sem.at[0]).start()
    for r in range(rows):
        pltpu.make_async_copy(c_in.at[:, r, 0], c.at[HALO + r], in_sem.at[1]).start()

    def own_rows(ref):
        return ref.at[pl.ds(HALO, rows)]

    blank = jnp.zeros((HALO, ch, cols), F32)
    for ref in (u, c):
        ref[pl.ds(0, HALO)] = blank
        ref[pl.ds(HALO + rows, HALO)] = blank
    blank16 = jnp.zeros((HALO, ch, cols), BF16)
    for ph in range(2 * ITERS):
        recvx[ph, pl.ds(0, HALO)] = blank16
        recvx[ph, pl.ds(HALO + rows, HALO)] = blank16

    barrier = pltpu.get_barrier_semaphore()

    def greet(i):
        pl.semaphore_signal(barrier, inc=1, device_id={"layer": partner(i)}, device_id_type=MESH)
    loop(1, nl, greet)

    def greet_space(i):
        pl.semaphore_signal(barrier, inc=1, device_id={"space": neighbour(i)}, device_id_type=MESH)
    loop(1, ns, greet_space)

    for ref in (y0, y1):
        for e in (0, 1, 2, ext - 1, ext, ext + 1):
            ref[e] = jnp.zeros((3 * ch, cols), F32)

    def halves(matrix):
        high = matrix.astype(BF16)
        low = (matrix - high.astype(F32)).astype(BF16)
        return jnp.concatenate([high, low], axis=1)

    in_w.wait()
    summed = w[0, 0].astype(F32)
    for tap in range(1, 9):
        summed = summed + w[0, tap].astype(F32)
    mb[me] = halves(2 * step_size * summed)
    for layer in range(2):
        for ty in range(3):
            wf[layer, ty * ch:(ty + 1) * ch] = jnp.concatenate(
                [w[layer, 3 * ty + tx] for tx in range(3)], axis=1)

    pltpu.make_async_copy(own_rows(u), own_rows(u), in_sem.at[0]).wait()
    pl.semaphore_wait(barrier, nl - 1 + ns - 1)

    def b_copy(i, source):
        k = partner(i)
        return pltpu.make_async_remote_copy(
            src_ref=mb.at[source], dst_ref=mb.at[source], send_sem=b_send.at[k],
            recv_sem=b_recv.at[source], device_id={"layer": k}, device_id_type=MESH)

    up_device = {"space": lax.rem(space + ns - 1, ns)}
    down_device = {"space": lax.rem(space + 1, ns)}

    def edge_copies(ref, width, send, recv):
        up = pltpu.make_async_remote_copy(
            src_ref=ref.at[pl.ds(HALO, width)], dst_ref=ref.at[pl.ds(HALO + rows, width)],
            send_sem=send.at[0], recv_sem=recv.at[1], device_id=up_device, device_id_type=MESH)
        down = pltpu.make_async_remote_copy(
            src_ref=ref.at[pl.ds(HALO + rows - width, width)],
            dst_ref=ref.at[pl.ds(HALO - width, width)],
            send_sem=send.at[1], recv_sem=recv.at[0], device_id=down_device, device_id_type=MESH)
        return up, down

    def edge_start(copies):
        up, down = copies
        pl.when(has_up)(up.start)
        pl.when(has_down)(down.start)

    def edge_wait(copies):
        up, down = copies

        @pl.when(has_up)
        def _():
            up.wait_send()
            down.wait_recv()

        @pl.when(has_down)
        def _():
            down.wait_send()
            up.wait_recv()

    edge_start(edge_copies(u, HALO, uh_send, uh_recv))

    def send_b(i):
        b_copy(i, me).start()
    loop(1, nl, send_b)

    lane = lax.broadcasted_iota(jnp.int32, (ch, cols), 1)
    not_first = lane > 0
    not_last = lane < cols - 1

    def shifted(v):
        left = jnp.where(not_first, pltpu.roll(v, 1, 1), 0.0)
        right = jnp.where(not_last, pltpu.roll(v, cols - 1, 1), 0.0)
        return jnp.concatenate([left.astype(BF16), v.astype(BF16), right.astype(BF16)], axis=0)

    def inside(e):
        return jnp.logical_and(
            jnp.logical_or(e >= HALO, has_up), jnp.logical_or(e < HALO + rows, has_down))

    def convolve(which, value, weight, y, keep=None):
        matrix = weight[...]
        values = [(value(2 * p), value(2 * p + 1)) for p in which]
        stacked = [
            jnp.concatenate([shifted(low), shifted(high)], axis=1) for low, high in values]
        products = [jnp.dot(matrix, x, preferred_element_type=F32) for x in stacked]
        for p, x, product in zip(which, stacked, products):
            if keep is not None:
                keep[p] = x
            y[2 * p + 1] = product[:, :cols]
            y[2 * p + 2] = product[:, cols:]

    def gathered(y, e):
        return y[e, 0:ch] + y[e + 1, ch:2 * ch] + y[e + 2, 2 * ch:3 * ch]

    def q_copy(ph, r, source):
        return pltpu.make_async_remote_copy(
            src_ref=sendq.at[ph, r], dst_ref=recvq.at[ph, source],
            send_sem=q_send.at[r], recv_sem=q_recv.at[ph, source],
            device_id={"layer": r}, device_id_type=MESH)

    def give_q(ph, which, value):
        for p in which:
            for e in (2 * p, 2 * p + 1):
                r = e - HALO
                entry = value(e)
                if ph % ITERS:
                    entry = entry - sendq[ph - 1, r].astype(F32)
                sendq[ph, r] = entry.astype(BF16)
        for p in which:
            for r in (2 * p - HALO, 2 * p + 1 - HALO):
                pl.when(r != me)(lambda r=r: q_copy(ph, r, me).start())

    def wait_q_sent(ph):
        def one(i):
            q_copy(ph, partner(i), me).wait_send()
        loop(1, nl, one)

    def x_copy(ph, k, row):
        return pltpu.make_async_remote_copy(
            src_ref=sendx.at[ph, k], dst_ref=recvx.at[ph, HALO + row],
            send_sem=x_send.at[k], recv_sem=x_recv.at[ph, row],
            device_id={"layer": k}, device_id_type=MESH)

    def wait_x_sent(ph):
        def one(i):
            x_copy(ph, partner(i), me).wait_send()
        loop(1, nl, one)

    def halo_copies(ph, far):
        def one(index, source, target, device):
            return pltpu.make_async_remote_copy(
                src_ref=recvx.at[ph, pl.ds(source, 2)], dst_ref=recvx.at[ph, pl.ds(target, 2)],
                send_sem=h_send.at[ph, index], recv_sem=h_recv.at[ph, index],
                device_id=device, device_id_type=MESH)
        last = HALO + rows
        up = [(0, one(0, HALO, last, up_device))]
        down = [(own - 1, one(2, last - 2, HALO - 2, down_device))]
        if far:
            up.append((1, one(1, HALO + 2, last + 2, up_device)))
            down.append((own - 2, one(3, last - 4, HALO - 4, down_device)))
        return up, down

    def sweep(arrival, far, edge, first_value, first_weight, second_value, second_weight,
              finish, keeps=(None, None), middle=None, spread=False):
        start = lax.div(lax.rem(me + nl - 1, nl), 2)

        def begin(m):
            places = [lax.rem(start + own - 2 * m - k, own) for k in range(2)]
            if arrival is not None:
                up, down = halo_copies(arrival, far)
                for place in places:
                    for row in (2 * place, 2 * place + 1):
                        pl.when(row != me)(
                            lambda row=row: x_copy(arrival, row, row).wait_recv())
                    for at, copy in up:
                        pl.when(jnp.logical_and(place == at, has_up))(copy.start)
                    for at, copy in down:
                        pl.when(jnp.logical_and(place == at, has_down))(copy.start)
            convolve([HALO // 2 + place for place in places],
                     first_value, first_weight, y0, keeps[0])
        loop(0, own // 2, begin)
        if arrival is None:
            edge_wait(edge)
        else:
            up, down = halo_copies(arrival, far)

            @pl.when(has_up)
            def _():
                for at, copy in up:
                    copy.wait_send()
                for at, copy in down:
                    copy.wait_recv()

            @pl.when(has_down)
            def _():
                for at, copy in down:
                    copy.wait_send()
                for at, copy in up:
                    copy.wait_recv()
        if spread:
            convolve([0, 1, pairs - 2, pairs - 1], first_value, first_weight, y0, keeps[0])
        else:
            convolve([1, pairs - 2], first_value, first_weight, y0, keeps[0])
            if far:
                for e in (0, 1, ext - 2, ext - 1):
                    first_value(e)
        if middle is not None:
            middle()

        def ring(n):
            return HALO // 2 + lax.rem(lax.div(me, 2) + own - 1 + n, own)
        outer = [0, 1, pairs - 2, pairs - 1] if spread else [1, pairs - 2]
        convolve(outer, second_value, second_weight, y1, keeps[1])
        convolve([ring(0), ring(1)], second_value, second_weight, y1, keeps[1])
        convolve([ring(2), ring(3)], second_value, second_weight, y1, keeps[1])

        def more(m):
            finish([ring(2 * m - 3), ring(2 * m - 2)])
            convolve([ring(2 * m), ring(2 * m + 1)], second_value, second_weight, y1, keeps[1])
        loop(2, own // 2, more)
        finish([ring(own - 3), ring(own - 2)])
        finish([ring(own - 1), ring(0)])

    def mixed(matrices, state):
        high = state.astype(BF16)
        low = (state - high.astype(F32)).astype(BF16)
        return jnp.dot(
            jnp.concatenate([matrices, matrices], axis=1),
            jnp.concatenate([high, high, low, low], axis=0), preferred_element_type=F32)

    def prepare(matrices, products):
        def one(g):
            total = [None] * 2
            for k in range(GROUP):
                for t in range(2):
                    at = GROUP * (2 * g + t) + k
                    matrix = matrices[at]
                    plain = matrix[:, :ch].astype(F32) + matrix[:, ch:].astype(F32)
                    if k == 0:
                        total[t] = plain
                    else:
                        total[t] = total[t] + plain + mixed(matrix, total[t])
                    products[2 * g + t, pl.ds(k * ch, ch)] = halves(total[t])
        loop(0, groups // 2, one)

    def scan(ph, matrices, products, reverse):
        blocks = groups // 2
        size = 2 * GROUP

        def section(i):
            return nl - 1 - i if reverse else i

        def shift(i):
            j = section(i)
            value = recvq[ph, j].astype(F32)
            if ph % ITERS:
                following = section(jnp.minimum(i + 1, nl - 1))
                value = (value + recvq[ph - 1, j].astype(F32)
                         + sendx[ph - 1, j].astype(F32) - sendx[ph - 1, following].astype(F32))
            return value

        def within(n):
            block = lax.rem(lax.div(lax.rem(me + nl - 1, nl), size) + 2 * blocks - 1 - n, blocks)

            def arrive(k):
                j = block * size + k
                pl.when(j != me)(lambda: q_copy(ph, j, j).wait_recv())
            loop(0, size, arrive)
            if reverse:
                block = blocks - 1 - block
            state = [None] * 2
            for k in range(GROUP):
                for t in range(2):
                    i = block * size + t * GROUP + k
                    value = shift(i)
                    if k > 0:
                        value = value + state[t] + mixed(matrices[i], state[t])
                    state[t] = value
                    ys[i] = value
        loop(0, blocks, within)

        entering = [jnp.zeros((ch, cols), F32), ys[GROUP - 1]]
        for g in range(1, groups - 1):
            state = entering[g]
            entering.append(
                ys[GROUP * g + GROUP - 1] + state
                + mixed(products[g, pl.ds((GROUP - 1) * ch, ch)], state))
        for g in range(groups):
            ys[GROUP * g + GROUP - 1] = entering[g]

        def spread_group(n):
            targets = []
            for t in range(2):
                g = lax.rem(lax.div(me, GROUP) + 2 * n + t, groups)
                if reverse:
                    g = groups - 1 - g
                state = ys[GROUP * g + GROUP - 1]
                change = mixed(products[g, pl.ds(0, (GROUP - 1) * ch)], state)
                results = [state]
                for k in range(GROUP - 1):
                    results.append(ys[GROUP * g + k] + state + change[k * ch:(k + 1) * ch])
                for k in range(GROUP):
                    j = section(GROUP * g + k)
                    sendx[ph, j] = results[k].astype(BF16)
                    targets.append(j)
            for j in targets:
                pl.when(j != me)(lambda j=j: x_copy(ph, j, me).start())
        loop(0, groups // 2, spread_group)
        recvx[ph, HALO + me] = sendx[ph, me]

    c_edge = edge_copies(c, 2, ch_send, ch_recv)

    def forward_first(ph, before):
        def value(e):
            if ph is None:
                return u[e]
            new = before[e] + recvx[ph, e].astype(F32)
            s[e] = new
            return new
        return value

    def forward_second(state):
        def value(e):
            tangent = jnp.tanh(gathered(y0, e))
            t0[e] = tangent
            return jnp.where(inside(e), state[e] + step_size * tangent, 0.0)
        return value

    def finish_forward(ph):
        def value(e):
            return step_size * (t0[e] + jnp.tanh(gathered(y1, e)))
        return lambda which: give_q(ph, which, value)

    sweep(None, False, edge_copies(u, HALO, uh_send, uh_recv), forward_first(None, None),
          wf.at[0], forward_second(u), wf.at[1], finish_forward(0))
    recvq[0, me] = sendq[0, me]

    pltpu.make_async_copy(own_rows(c), own_rows(c), in_sem.at[1]).wait()
    edge_start(c_edge)

    def settle_b(i):
        b_copy(i, me).wait_send()
        b_copy(i, partner(i)).wait_recv()
    loop(1, nl, settle_b)
    prepare(mb, fwd_p)
    scan(0, mb, fwd_p, False)
    wait_q_sent(0)

    sweep(0, True, None, forward_first(0, u), wf.at[0], forward_second(s), wf.at[1],
          finish_forward(1))
    recvq[1, me] = sendq[1, me]
    wait_x_sent(0)
    scan(1, mb, fwd_p, False)
    wait_q_sent(1)

    for layer in range(2):
        for ty in range(3):
            wb[layer, ty * ch:(ty + 1) * ch] = jnp.concatenate(
                [w[layer, 8 - 3 * ty - tx].astype(F32).T for tx in range(3)], axis=1).astype(BF16)

    def transpose_b(i):
        matrix = mb[nl - 1 - i].astype(F32).T
        rev_m[i] = jnp.concatenate([matrix[:ch], matrix[ch:]], axis=1).astype(BF16)
    loop(0, nl, transpose_b)
    prepare(rev_m, rev_p)

    def finish_last(which):
        for p in which:
            for e in (2 * p, 2 * p + 1):
                t1[e] = jnp.tanh(gathered(y1, e))
    sweep(1, True, None, forward_first(1, s), wf.at[0], forward_second(s), wf.at[1],
          finish_last, keeps=(x0, x1), spread=True)
    finish_last([1, pairs - 2])
    wait_x_sent(1)
    for r in range(rows):
        pltpu.make_async_copy(s.at[HALO + r], states_out.at[:, r, 0], out_sem.at[0]).start()

    def scaled(tangent, value):
        return step_size * (1.0 - tangent * tangent) * value

    def adjoint_first(ph, before, keep):
        def value(e):
            if ph is None:
                new = c[e]
            else:
                new = before[e] + recvx[ph, e].astype(F32)
                a[e] = new
            new = scaled(t1[e], new)
            if keep:
                d1[e] = new.astype(BF16)
            return new
        return value

    def adjoint_second(state, keep):
        def value(e):
            after = state[e] + gathered(y0, e)
            if keep:
                a1[e] = after
            new = jnp.where(inside(e), scaled(t0[e], after), 0.0)
            if keep:
                d0[e] = new.astype(BF16)
            return new
        return value

    def finish_adjoint(ph):
        def value(e):
            return gathered(y0, e) + gathered(y1, e)
        return lambda which: give_q(ph, which, value)

    sweep(None, False, c_edge, adjoint_first(None, None, False), wb.at[1],
          adjoint_second(c, False), wb.at[0], finish_adjoint(2))
    recvq[2, me] = sendq[2, me]
    scan(2, rev_m, rev_p, True)
    wait_q_sent(2)
    sweep(2, False, None, adjoint_first(2, c, False), wb.at[1],
          adjoint_second(a, False), wb.at[0], finish_adjoint(3))
    recvq[3, me] = sendq[3, me]
    wait_x_sent(2)
    scan(3, rev_m, rev_p, True)
    wait_q_sent(3)

    quarter = 3 * ch // ns

    def gradient(layer, d, x):
        d[pl.ds(0, HALO)] = blank16
        d[pl.ds(HALO + rows, HALO)] = blank16

        def one(m, total):
            which = [1 + 3 * m + k for k in range(3)]
            left, right = [], []
            for p in which:
                for e in (2 * p, 2 * p + 1):
                    left.append(jnp.concatenate([d[e + 1], d[e], d[e - 1]], axis=0))
                right.append(x[p])
            return total + lax.dot_general(
                jnp.concatenate(left, axis=1), jnp.concatenate(right, axis=1),
                (((1,), (1,)), ((), ())), preferred_element_type=F32)
        grad[layer] = lax.fori_loop(
            0, (pairs - 2) // 3, one, jnp.zeros((3 * ch, 3 * ch), F32))
        for i in range(1, ns):
            g_copy(layer, i, space).start()

    def part(index):
        return pl.ds(pl.multiple_of(index * quarter, quarter), quarter)

    def g_copy(layer, i, source):
        k = neighbour(i)
        return pltpu.make_async_remote_copy(
            src_ref=grad.at[layer, part(k)], dst_ref=grecv.at[layer, source],
            send_sem=g_send.at[layer, k], recv_sem=g_recv.at[layer, source],
            device_id={"space": k}, device_id_type=MESH)

    def r_copy(layer, i, source):
        k = neighbour(i)
        return pltpu.make_async_remote_copy(
            src_ref=gsum.at[layer, part(source)], dst_ref=gsum.at[layer, part(source)],
            send_sem=r_send.at[layer, k], recv_sem=r_recv.at[layer, source],
            device_id={"space": k}, device_id_type=MESH)

    def reduce_part(layer):
        total = grad[layer, part(space)]
        for i in range(1, ns):
            g_copy(layer, i, neighbour(i)).wait_recv()
            total = total + grecv[layer, neighbour(i)]
        gsum[layer, part(space)] = total
        for i in range(1, ns):
            r_copy(layer, i, space).start()

    def collect(layer):
        for i in range(1, ns):
            g_copy(layer, i, space).wait_send()
            r_copy(layer, i, neighbour(i)).wait_recv()
            r_copy(layer, i, space).wait_send()
        for ty in range(3):
            for tx in range(3):
                gout[9 * layer + 3 * ty + tx] = (
                    gsum[layer, ty * ch:(ty + 1) * ch, tx * ch:(tx + 1) * ch])

    def finish_start(which):
        for p in which:
            for e in (2 * p, 2 * p + 1):
                a1[e] = a1[e] + gathered(y1, e)

    sweep(3, False, None, adjoint_first(3, a, True), wb.at[1], adjoint_second(a, True), wb.at[0],
          finish_start, middle=lambda: gradient(1, d1, x1))
    for r in range(rows):
        pltpu.make_async_copy(a1.at[HALO + r], adj_out.at[:, r, 0], out_sem.at[1]).start()
    gradient(0, d0, x0)
    wait_x_sent(3)
    reduce_part(1)
    reduce_part(0)
    collect(1)
    collect(0)
    grads = pltpu.make_async_copy(gout, grads_out, out_sem.at[2])
    grads.start()
    pltpu.make_async_copy(own_rows(s), own_rows(s), out_sem.at[0]).wait()
    pltpu.make_async_copy(own_rows(a1), own_rows(a1), out_sem.at[1]).wait()
    grads.wait()


def per_device(image_features, output_cotangent, conv_weights):
    nl, ns = lax.axis_size("layer"), lax.axis_size("space")
    layers, _, ch, _ = conv_weights.shape
    _, _, rows, cols = image_features.shape
    assert rows == nl and layers == 2 and cols == 2 * ch
    step_size = HORIZON / (layers * nl)
    ext = rows + 2 * HALO
    vmem = pltpu.VMEM

    def field(kind):
        return vmem((ext, ch, cols), kind)
    any_spec = pl.BlockSpec(memory_space=pl.ANY)
    dma = pltpu.SemaphoreType.DMA
    phases = 2 * ITERS
    states, starts, grads = pl.pallas_call(
        functools.partial(kernel, nl, ns, rows, ch, cols, step_size),
        out_shape=(
            jax.ShapeDtypeStruct((ch, rows, 1, cols), F32),
            jax.ShapeDtypeStruct((ch, rows, 1, cols), F32),
            jax.ShapeDtypeStruct((layers * 9, ch, ch), F32),
        ),
        in_specs=[any_spec, any_spec, any_spec],
        out_specs=(any_spec, any_spec, any_spec),
        scratch_shapes=[
            field(F32), field(F32), field(F32), field(F32), field(F32), field(F32), field(F32),
            vmem((ext + 2, 3 * ch, cols), F32),
            vmem((ext + 2, 3 * ch, cols), F32),
            vmem((ext // 2, 3 * ch, 2 * cols), BF16),
            vmem((ext // 2, 3 * ch, 2 * cols), BF16),
            field(BF16), field(BF16),
            vmem((phases, rows, ch, cols), BF16),
            vmem((phases, nl, ch, cols), BF16),
            vmem((phases, nl, ch, cols), BF16),
            vmem((phases, ext, ch, cols), BF16),
            vmem((layers, 9, ch, ch), BF16),
            vmem((layers, 3 * ch, 3 * ch), BF16),
            vmem((layers, 3 * ch, 3 * ch), BF16),
            vmem((nl, ch, 2 * ch), BF16),
            vmem((nl, ch, 2 * ch), BF16),
            vmem((nl // GROUP, GROUP * ch, 2 * ch), BF16),
            vmem((nl // GROUP, GROUP * ch, 2 * ch), BF16),
            vmem((nl, ch, cols), F32),
            vmem((layers, 3 * ch, 3 * ch), F32),
            vmem((layers, ns, 3 * ch // ns, 3 * ch), F32),
            vmem((layers, 3 * ch, 3 * ch), F32),
            vmem((layers * 9, ch, ch), F32),
            dma((3,)), dma((3,)), dma((2,)), dma((2,)), dma((2,)), dma((2,)),
            dma((nl,)), dma((nl,)),
            dma((nl,)), dma((phases, nl)), dma((nl,)), dma((phases, nl)),
            dma((phases, 4)), dma((phases, 4)),
            dma((layers, ns)), dma((layers, ns)), dma((layers, ns)), dma((layers, ns)),
        ],
        compiler_params=pltpu.CompilerParams(
            collective_id=0, has_side_effects=True, vmem_limit_bytes=56 * 1024 * 1024),
        name="mgrit",
    )(
        image_features.reshape(ch, rows, 1, cols),
        output_cotangent.reshape(ch, rows, 1, cols),
        conv_weights,
    )
    return (
        states.reshape(1, 1, ch, rows, cols),
        starts.reshape(1, 1, ch, rows, cols),
        grads.reshape(layers, 9, ch, ch),
    )


def solution(mesh):
    placed = (
        P(None, None, "space", None),
        P(None, None, "space", None),
        P("layer", None, None, None),
    )
    return jax.shard_map(
        per_device,
        mesh=mesh,
        in_specs=placed,
        out_specs=(
            P("layer", None, None, "space", None),
            P("layer", None, None, "space", None),
            P("layer", None, None, None),
        ),
        check_vma=False,
    )
```

time: 1180 us -> 148 us (0.13); the launches traced: 1160 us -> 148 us
  waiting for transfers between devices: 564 us -> 0 us
  matrix products: 237 us -> 0 us
  blocking collectives: 150 us -> 0 us
  Pallas kernels: 0 us -> 143 us
  local copies, waits for them, and re-layouts: 120 us -> 4.61 us
  starting transfers between devices: 56.9 us -> 0 us
  between operations: 15.7 us -> 0.65 us
    all_gather x4 -> x0, waiting for transfers between devices: 487 us -> none  [entering(): gathered = jax.tree.map(lambda a: lax.all_gather(a, axis), part)]
    dot_general x146 -> x0, matrix products: 237 us -> none  [the longest x70 157 us: mix_channels(): return jnp.einsum('oc,bcrw->borw', matrix, field_state, precision=highest)]
    all_gather x2 -> x0, blocking collectives: 150 us -> none  [entering(): gathered = jax.tree.map(lambda a: lax.all_gather(a, axis), part)]
    pallas_call x0 -> x1, Pallas kernels: none -> 143 us  [per_device(): pl.pallas_call(functools.partial(kernel, nl, ns, rows, ch, cols, step_siz...]
    dynamic_slice x62 -> x0, local copies, waits for them, and re-layouts: 80.5 us -> none  [one(): lax.dynamic_index_in_dim(a, source, 0, False)]
    ppermute x24 -> x0, starting transfers between devices: 56.7 us -> none  [the longest x12 40.4 us: extended(): lax.ppermute(lax.slice_in_dim(block, block.shape[dim] - width, None, axis...]
    ppermute x24 -> x0, waiting for transfers between devices: 44 us -> none  [the longest x12 43.3 us: extended(): lax.ppermute(lax.slice_in_dim(block, 0, width, axis=dim), axis, backward)]
    psum x1 -> x0, waiting for transfers between devices: 32.8 us -> none  [per_device(): weight_grads = lax.psum(local_grads, 'space')]
  transfers between devices with their start and end apart: 29 -> 0, of which waited for: 21 -> 0; matrix products, arithmetic and copies ran while one was open for 1% -> 0% of each run, Pallas kernels for 0% -> 0%
where the time goes in v2:
time: 148 us
  Pallas kernels  143 us (97%)
  local copies, waits for them, and re-layouts  4.61 us (3%)
    pallas_call x1, Pallas kernels, per_device(): pl.pallas_call(functools.partial(kernel, nl, ns, rows, ch, cols, step_siz...  143 us
    unnamed x7, local copies, waits for them, and re-layouts  4.61 us

profile of v2, /device:TPU:0, one launch (start us, length us, event | category | flops | bytes accessed | tf_op | source)
XLA Modules:
  0.0 148.1 jit_solution(4824676652602208287)
XLA Ops:
  0.6 142.9 %mgrit.1 = (f32[64,32,1,128]{3,2,1,0:T(1,128)}, f32[64,32,1,128]{3,2,1,0:T(1,128)}, f32[18,64,64]{2,1,0:T(8,128)}) custom-call(f32[64,32,1,128]{3,2,1,0:T(1,128)} %bitcast.5, f32[64,32,1,128]{3,2,1,0:T(1,128)} %bitcast.6, bf16[2,9,64,64]{3,2,1,0:T(8,128)(2,1)} %w_in.1), custom_call_target="tpu_custom_call" | custom-call | tf_op jit(solution)/shard_map/mgrit/pallas_call | solution.py:573
  143.5 0.0 copy-start
  143.5 2.4 %copy.9 = f32[1,1,64,32,128]{4,3,2,1,0:T(8,128)} copy(f32[1,1,64,32,128]{4,3,2,1,0:T(8,128)} %bitcast.8) | data formatting | bytes 2097152
  145.9 0.0 copy-done
  145.9 0.0 copy-start.1
  145.9 1.0 copy.10
  146.9 0.5 copy-done.1
  147.3 0.8 copy.11
Async XLA Ops:
  143.5 2.4 %copy-start = (f32[64,32,1,128]{3,2,1,0:T(1,128)S(1)}, f32[64,32,1,128]{3,2,1,0:T(1,128)}, u32[]{:S(2)}) copy-start(f32[64,32,1,128]{3,2,1,0:T(1,128)} %get-tuple-element.7) | copy-start | bytes 3145732
  145.9 1.4 copy-start.1

commit v3 on v2

--- a/solution.py
+++ b/solution.py
@@ -33,6 +33,8 @@
     pairs = ext // 2
     own = rows // 2
     groups = nl // GROUP
+    spread_by = nl // 4
+    my_row = lax.rem(me, spread_by) * 4 + lax.div(me, spread_by)
     has_up = space > 0
     has_down = space < ns - 1
 
@@ -47,6 +49,19 @@
 
     def neighbour(i):
         return lax.rem(space + i, ns)
+
+    def scanner(r):
+        return lax.rem(r, 4) * spread_by + lax.div(r, 4)
+
+    barrier = pltpu.get_barrier_semaphore()
+
+    def greet(i):
+        pl.semaphore_signal(barrier, inc=1, device_id={"layer": partner(i)}, device_id_type=MESH)
+    loop(1, nl, greet)
+
+    def greet_space(i):
+        pl.semaphore_signal(barrier, inc=1, device_id={"space": neighbour(i)}, device_id_type=MESH)
+    loop(1, ns, greet_space)
 
     in_w = pltpu.make_async_copy(w_in, w, in_sem.at[2])
     in_w.start()
@@ -59,23 +74,18 @@
         return ref.at[pl.ds(HALO, rows)]
 
     blank = jnp.zeros((HALO, ch, cols), F32)
-    for ref in (u, c):
-        ref[pl.ds(0, HALO)] = blank
-        ref[pl.ds(HALO + rows, HALO)] = blank
     blank16 = jnp.zeros((HALO, ch, cols), BF16)
-    for ph in range(2 * ITERS):
-        recvx[ph, pl.ds(0, HALO)] = blank16
-        recvx[ph, pl.ds(HALO + rows, HALO)] = blank16
-
-    barrier = pltpu.get_barrier_semaphore()
-
-    def greet(i):
-        pl.semaphore_signal(barrier, inc=1, device_id={"layer": partner(i)}, device_id_type=MESH)
-    loop(1, nl, greet)
-
-    def greet_space(i):
-        pl.semaphore_signal(barrier, inc=1, device_id={"space": neighbour(i)}, device_id_type=MESH)
-    loop(1, ns, greet_space)
+
+    def clear(part):
+        for ref in (u, c):
+            ref[part] = blank
+        for ph in range(2 * ITERS):
+            recvx[ph, part] = blank16
+
+    pl.when(space == 0)(lambda: clear(pl.ds(0, HALO)))
+    pl.when(space == ns - 1)(lambda: clear(pl.ds(HALO + rows, HALO)))
+    for part in (pl.ds(0, HALO - 2), pl.ds(HALO + rows + 2, HALO - 2)):
+        c[part] = blank[:HALO - 2]
 
     for ref in (y0, y1):
         for e in (0, 1, 2, ext - 1, ext, ext + 1):
@@ -136,11 +146,21 @@
             down.wait_send()
             up.wait_recv()
 
-    edge_start(edge_copies(u, HALO, uh_send, uh_recv))
+    far_u = (
+        pltpu.make_async_remote_copy(
+            src_ref=u.at[pl.ds(HALO + 2, 2)], dst_ref=u.at[pl.ds(HALO + rows + 2, 2)],
+            send_sem=uh_send.at[2], recv_sem=uh_recv.at[3], device_id=up_device,
+            device_id_type=MESH),
+        pltpu.make_async_remote_copy(
+            src_ref=u.at[pl.ds(HALO + rows - 4, 2)], dst_ref=u.at[pl.ds(0, 2)],
+            send_sem=uh_send.at[3], recv_sem=uh_recv.at[2], device_id=down_device,
+            device_id_type=MESH))
+    edge_start(edge_copies(u, 2, uh_send, uh_recv))
 
     def send_b(i):
         b_copy(i, me).start()
     loop(1, nl, send_b)
+    edge_start(far_u)
 
     lane = lax.broadcasted_iota(jnp.int32, (ch, cols), 1)
     not_first = lane > 0
@@ -174,7 +194,7 @@
         return pltpu.make_async_remote_copy(
             src_ref=sendq.at[ph, r], dst_ref=recvq.at[ph, source],
             send_sem=q_send.at[r], recv_sem=q_recv.at[ph, source],
-            device_id={"layer": r}, device_id_type=MESH)
+            device_id={"layer": scanner(r)}, device_id_type=MESH)
 
     def give_q(ph, which, value):
         for p in which:
@@ -186,12 +206,12 @@
                 sendq[ph, r] = entry.astype(BF16)
         for p in which:
             for r in (2 * p - HALO, 2 * p + 1 - HALO):
-                pl.when(r != me)(lambda r=r: q_copy(ph, r, me).start())
+                pl.when(r != my_row)(lambda r=r: q_copy(ph, r, me).start())
 
     def wait_q_sent(ph):
         def one(i):
-            q_copy(ph, partner(i), me).wait_send()
-        loop(1, nl, one)
+            pl.when(i != my_row)(lambda: q_copy(ph, i, me).wait_send())
+        loop(0, rows, one)
 
     def x_copy(ph, k, row):
         return pltpu.make_async_remote_copy(
@@ -201,7 +221,7 @@
 
     def wait_x_sent(ph):
         def one(i):
-            x_copy(ph, partner(i), me).wait_send()
+            x_copy(ph, partner(i), my_row).wait_send()
         loop(1, nl, one)
 
     def halo_copies(ph, far):
@@ -218,28 +238,32 @@
             down.append((own - 2, one(3, last - 4, HALO - 4, down_device)))
         return up, down
 
+    inner = max(own - 4, 0)
+    first_own = HALO // 2
+
     def sweep(arrival, far, edge, first_value, first_weight, second_value, second_weight,
-              finish, keeps=(None, None), middle=None, spread=False):
-        start = lax.div(lax.rem(me + nl - 1, nl), 2)
-
+              finish, keeps=(None, None), spread=False, last=None):
         def begin(m):
-            places = [lax.rem(start + own - 2 * m - k, own) for k in range(2)]
+            block = lax.rem(lax.div(me, GROUP) + groups - m, groups)
+            places = [2 * block, 2 * block + 1]
             if arrival is not None:
                 up, down = halo_copies(arrival, far)
                 for place in places:
                     for row in (2 * place, 2 * place + 1):
-                        pl.when(row != me)(
+                        pl.when(row != my_row)(
                             lambda row=row: x_copy(arrival, row, row).wait_recv())
                     for at, copy in up:
                         pl.when(jnp.logical_and(place == at, has_up))(copy.start)
                     for at, copy in down:
                         pl.when(jnp.logical_and(place == at, has_down))(copy.start)
-            convolve([HALO // 2 + place for place in places],
+            convolve([first_own + place for place in places],
                      first_value, first_weight, y0, keeps[0])
         loop(0, own // 2, begin)
-        if arrival is None:
-            edge_wait(edge)
-        else:
+
+        def settle():
+            if arrival is None:
+                edge_wait(edge)
+                return
             up, down = halo_copies(arrival, far)
 
             @pl.when(has_up)
@@ -255,29 +279,48 @@
                     copy.wait_send()
                 for at, copy in up:
                     copy.wait_recv()
-        if spread:
-            convolve([0, 1, pairs - 2, pairs - 1], first_value, first_weight, y0, keeps[0])
-        else:
+
+        def rim():
+            if spread:
+                convolve([0, 1, pairs - 2, pairs - 1], first_value, first_weight, y0, keeps[0])
+                return
             convolve([1, pairs - 2], first_value, first_weight, y0, keeps[0])
             if far:
                 for e in (0, 1, ext - 2, ext - 1):
                     first_value(e)
-        if middle is not None:
-            middle()
+
+        if last is not None:
+            last(settle, rim)
+            return
 
         def ring(n):
-            return HALO // 2 + lax.rem(lax.div(me, 2) + own - 1 + n, own)
-        outer = [0, 1, pairs - 2, pairs - 1] if spread else [1, pairs - 2]
-        convolve(outer, second_value, second_weight, y1, keeps[1])
-        convolve([ring(0), ring(1)], second_value, second_weight, y1, keeps[1])
-        convolve([ring(2), ring(3)], second_value, second_weight, y1, keeps[1])
-
-        def more(m):
-            finish([ring(2 * m - 3), ring(2 * m - 2)])
-            convolve([ring(2 * m), ring(2 * m + 1)], second_value, second_weight, y1, keeps[1])
-        loop(2, own // 2, more)
-        finish([ring(own - 3), ring(own - 2)])
-        finish([ring(own - 1), ring(0)])
+            start = lax.div(lax.div(me, 2) * inner, own)
+            return first_own + 2 + lax.rem(start + inner - 1 + n, inner)
+
+        def second(which):
+            convolve(which, second_value, second_weight, y1, keeps[1])
+
+        second([first_own + 1, pairs - first_own - 2])
+        if inner:
+            second([ring(0), ring(1)])
+            second([ring(2), ring(3)])
+
+            def more(m):
+                finish([ring(2 * m - 3), ring(2 * m - 2)])
+                second([ring(2 * m), ring(2 * m + 1)])
+            loop(2, inner // 2, more)
+            finish([ring(inner - 3), ring(inner - 2)])
+            finish([ring(inner - 1), ring(0)])
+        settle()
+        rim()
+        if spread:
+            second([0, 1, 2])
+            second([pairs - 3, pairs - 2, pairs - 1])
+            finish([1, pairs - 2])
+        else:
+            second([1, 2, pairs - 3, pairs - 2])
+        finish([2, 3])
+        finish([pairs - 4, pairs - 3])
 
     def mixed(matrices, state):
         high = state.astype(BF16)
@@ -287,24 +330,25 @@
             jnp.concatenate([high, high, low, low], axis=0), preferred_element_type=F32)
 
     def prepare(matrices, products):
-        def one(g):
-            total = [None] * 2
-            for k in range(GROUP):
-                for t in range(2):
-                    at = GROUP * (2 * g + t) + k
-                    matrix = matrices[at]
-                    plain = matrix[:, :ch].astype(F32) + matrix[:, ch:].astype(F32)
-                    if k == 0:
-                        total[t] = plain
-                    else:
-                        total[t] = total[t] + plain + mixed(matrix, total[t])
-                    products[2 * g + t, pl.ds(k * ch, ch)] = halves(total[t])
-        loop(0, groups // 2, one)
+        total = [None] * groups
+        for k in range(GROUP):
+            for g in range(groups):
+                matrix = matrices[GROUP * g + k]
+                plain = matrix[:, :ch].astype(F32) + matrix[:, ch:].astype(F32)
+                if k == 0:
+                    total[g] = plain
+                else:
+                    total[g] = total[g] + plain + mixed(matrix, total[g])
+                products[g, pl.ds(k * ch, ch)] = halves(total[g])
+        for level in range(2):
+            reach = 1 << level
+            before = list(total)
+            for g in range(2 * reach, groups - 1):
+                matrix = halves(before[g])
+                total[g] = before[g] + before[g - reach] + mixed(matrix, before[g - reach])
+                products[g, pl.ds((GROUP + level) * ch, ch)] = halves(total[g])
 
     def scan(ph, matrices, products, reverse):
-        blocks = groups // 2
-        size = 2 * GROUP
-
         def section(i):
             return nl - 1 - i if reverse else i
 
@@ -312,59 +356,57 @@
             j = section(i)
             value = recvq[ph, j].astype(F32)
             if ph % ITERS:
-                following = section(jnp.minimum(i + 1, nl - 1))
+                following = section(min(i + 1, nl - 1))
                 value = (value + recvq[ph - 1, j].astype(F32)
                          + sendx[ph - 1, j].astype(F32) - sendx[ph - 1, following].astype(F32))
             return value
 
-        def within(n):
-            block = lax.rem(lax.div(lax.rem(me + nl - 1, nl), size) + 2 * blocks - 1 - n, blocks)
-
-            def arrive(k):
-                j = block * size + k
-                pl.when(j != me)(lambda: q_copy(ph, j, j).wait_recv())
-            loop(0, size, arrive)
-            if reverse:
-                block = blocks - 1 - block
-            state = [None] * 2
-            for k in range(GROUP):
-                for t in range(2):
-                    i = block * size + t * GROUP + k
-                    value = shift(i)
-                    if k > 0:
-                        value = value + state[t] + mixed(matrices[i], state[t])
-                    state[t] = value
-                    ys[i] = value
-        loop(0, blocks, within)
-
-        entering = [jnp.zeros((ch, cols), F32), ys[GROUP - 1]]
-        for g in range(1, groups - 1):
-            state = entering[g]
-            entering.append(
-                ys[GROUP * g + GROUP - 1] + state
-                + mixed(products[g, pl.ds((GROUP - 1) * ch, ch)], state))
-        for g in range(groups):
-            ys[GROUP * g + GROUP - 1] = entering[g]
+        def arrive(j):
+            pl.when(j != me)(lambda: q_copy(ph, my_row, j).wait_recv())
+        loop(0, nl, arrive)
+
+        state = [None] * groups
+        for k in range(GROUP):
+            for g in range(groups):
+                i = GROUP * g + k
+                value = shift(i)
+                if k > 0:
+                    value = value + state[g] + mixed(matrices[i], state[g])
+                state[g] = value
+                ys[i] = value
+
+        reach = 1
+        level = 0
+        while reach < groups - 1:
+            before = list(state)
+            at = pl.ds((GROUP - 1 + level) * ch, ch)
+            for g in range(reach, groups - 1):
+                state[g] = before[g] + before[g - reach] + mixed(products[g, at], before[g - reach])
+            reach *= 2
+            level += 1
+        for g in range(1, groups):
+            ys[GROUP * g + GROUP - 1] = state[g - 1]
+        ys[GROUP - 1] = jnp.zeros((ch, cols), F32)
 
         def spread_group(n):
             targets = []
             for t in range(2):
-                g = lax.rem(lax.div(me, GROUP) + 2 * n + t, groups)
+                g = lax.rem(lax.div(my_row, GROUP) + 2 * n + t, groups)
                 if reverse:
                     g = groups - 1 - g
-                state = ys[GROUP * g + GROUP - 1]
-                change = mixed(products[g, pl.ds(0, (GROUP - 1) * ch)], state)
-                results = [state]
+                start = ys[GROUP * g + GROUP - 1]
+                change = mixed(products[g, pl.ds(0, (GROUP - 1) * ch)], start)
+                results = [start]
                 for k in range(GROUP - 1):
-                    results.append(ys[GROUP * g + k] + state + change[k * ch:(k + 1) * ch])
+                    results.append(ys[GROUP * g + k] + start + change[k * ch:(k + 1) * ch])
                 for k in range(GROUP):
                     j = section(GROUP * g + k)
                     sendx[ph, j] = results[k].astype(BF16)
                     targets.append(j)
             for j in targets:
-                pl.when(j != me)(lambda j=j: x_copy(ph, j, me).start())
+                pl.when(j != me)(lambda j=j: x_copy(ph, j, my_row).start())
         loop(0, groups // 2, spread_group)
-        recvx[ph, HALO + me] = sendx[ph, me]
+        recvx[ph, HALO + my_row] = sendx[ph, me]
 
     c_edge = edge_copies(c, 2, ch_send, ch_recv)
 
@@ -389,9 +431,9 @@
             return step_size * (t0[e] + jnp.tanh(gathered(y1, e)))
         return lambda which: give_q(ph, which, value)
 
-    sweep(None, False, edge_copies(u, HALO, uh_send, uh_recv), forward_first(None, None),
+    sweep(None, False, edge_copies(u, 2, uh_send, uh_recv), forward_first(None, None),
           wf.at[0], forward_second(u), wf.at[1], finish_forward(0))
-    recvq[0, me] = sendq[0, me]
+    recvq[0, me] = sendq[0, my_row]
 
     pltpu.make_async_copy(own_rows(c), own_rows(c), in_sem.at[1]).wait()
     edge_start(c_edge)
@@ -401,26 +443,28 @@
         b_copy(i, partner(i)).wait_recv()
     loop(1, nl, settle_b)
     prepare(mb, fwd_p)
+    edge_wait(far_u)
     scan(0, mb, fwd_p, False)
     wait_q_sent(0)
 
     sweep(0, True, None, forward_first(0, u), wf.at[0], forward_second(s), wf.at[1],
           finish_forward(1))
-    recvq[1, me] = sendq[1, me]
+    recvq[1, me] = sendq[1, my_row]
     wait_x_sent(0)
-    scan(1, mb, fwd_p, False)
-    wait_q_sent(1)
 
     for layer in range(2):
         for ty in range(3):
             wb[layer, ty * ch:(ty + 1) * ch] = jnp.concatenate(
                 [w[layer, 8 - 3 * ty - tx].astype(F32).T for tx in range(3)], axis=1).astype(BF16)
 
-    def transpose_b(i):
-        matrix = mb[nl - 1 - i].astype(F32).T
-        rev_m[i] = jnp.concatenate([matrix[:ch], matrix[ch:]], axis=1).astype(BF16)
-    loop(0, nl, transpose_b)
+    def transpose_b(m):
+        for i in range(4):
+            matrix = mb[nl - 1 - 4 * m - i].astype(F32).T
+            rev_m[4 * m + i] = jnp.concatenate([matrix[:ch], matrix[ch:]], axis=1).astype(BF16)
+    loop(0, nl // 4, transpose_b)
     prepare(rev_m, rev_p)
+    scan(1, mb, fwd_p, False)
+    wait_q_sent(1)
 
     def finish_last(which):
         for p in which:
@@ -428,7 +472,6 @@
                 t1[e] = jnp.tanh(gathered(y1, e))
     sweep(1, True, None, forward_first(1, s), wf.at[0], forward_second(s), wf.at[1],
           finish_last, keeps=(x0, x1), spread=True)
-    finish_last([1, pairs - 2])
     wait_x_sent(1)
     for r in range(rows):
         pltpu.make_async_copy(s.at[HALO + r], states_out.at[:, r, 0], out_sem.at[0]).start()
@@ -449,15 +492,10 @@
             return new
         return value
 
-    def adjoint_second(state, keep):
+    def adjoint_second(state):
         def value(e):
             after = state[e] + gathered(y0, e)
-            if keep:
-                a1[e] = after
-            new = jnp.where(inside(e), scaled(t0[e], after), 0.0)
-            if keep:
-                d0[e] = new.astype(BF16)
-            return new
+            return jnp.where(inside(e), scaled(t0[e], after), 0.0)
         return value
 
     def finish_adjoint(ph):
@@ -466,13 +504,13 @@
         return lambda which: give_q(ph, which, value)
 
     sweep(None, False, c_edge, adjoint_first(None, None, False), wb.at[1],
-          adjoint_second(c, False), wb.at[0], finish_adjoint(2))
-    recvq[2, me] = sendq[2, me]
+          adjoint_second(c), wb.at[0], finish_adjoint(2))
+    recvq[2, me] = sendq[2, my_row]
     scan(2, rev_m, rev_p, True)
     wait_q_sent(2)
     sweep(2, False, None, adjoint_first(2, c, False), wb.at[1],
-          adjoint_second(a, False), wb.at[0], finish_adjoint(3))
-    recvq[3, me] = sendq[3, me]
+          adjoint_second(a), wb.at[0], finish_adjoint(3))
+    recvq[3, me] = sendq[3, my_row]
     wait_x_sent(2)
     scan(3, rev_m, rev_p, True)
     wait_q_sent(3)
@@ -483,8 +521,10 @@
         d[pl.ds(0, HALO)] = blank16
         d[pl.ds(HALO + rows, HALO)] = blank16
 
+        many = 3 if (pairs - 2) % 3 == 0 else 2
+
         def one(m, total):
-            which = [1 + 3 * m + k for k in range(3)]
+            which = [1 + many * m + k for k in range(many)]
             left, right = [], []
             for p in which:
                 for e in (2 * p, 2 * p + 1):
@@ -494,7 +534,7 @@
                 jnp.concatenate(left, axis=1), jnp.concatenate(right, axis=1),
                 (((1,), (1,)), ((), ())), preferred_element_type=F32)
         grad[layer] = lax.fori_loop(
-            0, (pairs - 2) // 3, one, jnp.zeros((3 * ch, 3 * ch), F32))
+            0, (pairs - 2) // many, one, jnp.zeros((3 * ch, 3 * ch), F32))
         for i in range(1, ns):
             g_copy(layer, i, space).start()
 
@@ -534,16 +574,39 @@
                 gout[9 * layer + 3 * ty + tx] = (
                     gsum[layer, ty * ch:(ty + 1) * ch, tx * ch:(tx + 1) * ch])
 
-    def finish_start(which):
-        for p in which:
+    def last_steps(settle, rim):
+        gradient(1, d1, x1)
+        settle()
+        rim()
+
+        def scale(p):
             for e in (2 * p, 2 * p + 1):
-                a1[e] = a1[e] + gathered(y1, e)
-
-    sweep(3, False, None, adjoint_first(3, a, True), wb.at[1], adjoint_second(a, True), wb.at[0],
-          finish_start, middle=lambda: gradient(1, d1, x1))
+                after = a[e] + gathered(y0, e)
+                a1[e] = after
+                d0[e] = jnp.where(inside(e), scaled(t0[e], after), 0.0).astype(BF16)
+
+        def scale_two(m):
+            scale(1 + 2 * m)
+            scale(2 + 2 * m)
+        loop(0, (pairs - 2) // 2, scale_two)
+        top, bottom = d0[HALO - 1], d0[HALO + rows]
+        gradient(0, d0, x0)
+        d0[HALO - 1] = top
+        d0[HALO + rows] = bottom
+
+        def second(m):
+            convolve([1 + 2 * m, 2 + 2 * m], lambda e: d0[e].astype(F32), wb.at[0], y1)
+        loop(0, (pairs - 2) // 2, second)
+
+        def end(m):
+            for e in range(4):
+                at = HALO + 4 * m + e
+                a1[at] = a1[at] + gathered(y1, at)
+        loop(0, rows // 4, end)
+
+    sweep(3, False, None, adjoint_first(3, a, True), wb.at[1], None, None, None, last=last_steps)
     for r in range(rows):
         pltpu.make_async_copy(a1.at[HALO + r], adj_out.at[:, r, 0], out_sem.at[1]).start()
-    gradient(0, d0, x0)
     wait_x_sent(3)
     reduce_part(1)
     reduce_part(0)
@@ -554,6 +617,27 @@
     pltpu.make_async_copy(own_rows(s), own_rows(s), out_sem.at[0]).wait()
     pltpu.make_async_copy(own_rows(a1), own_rows(a1), out_sem.at[1]).wait()
     grads.wait()
+
+
+def publish_body(*refs):
+    half = len(refs) // 2
+    for source, target in zip(refs[:half], refs[half:]):
+        target[...] = source[...]
+
+
+def publish(*arrays):
+    steps = 2
+    specs = [
+        pl.BlockSpec((x.shape[0] // steps,) + x.shape[1:], lambda i, n=x.ndim: (i,) + (0,) * (n - 1))
+        for x in arrays]
+    return pl.pallas_call(
+        publish_body,
+        grid=(steps,),
+        out_shape=tuple(jax.ShapeDtypeStruct(x.shape, x.dtype) for x in arrays),
+        in_specs=specs,
+        out_specs=tuple(specs),
+        name="publish",
+    )(*arrays)
 
 
 def per_device(image_features, output_cotangent, conv_weights):
@@ -595,14 +679,14 @@
             vmem((layers, 3 * ch, 3 * ch), BF16),
             vmem((nl, ch, 2 * ch), BF16),
             vmem((nl, ch, 2 * ch), BF16),
-            vmem((nl // GROUP, GROUP * ch, 2 * ch), BF16),
-            vmem((nl // GROUP, GROUP * ch, 2 * ch), BF16),
+            vmem((nl // GROUP, (GROUP + 2) * ch, 2 * ch), BF16),
+            vmem((nl // GROUP, (GROUP + 2) * ch, 2 * ch), BF16),
             vmem((nl, ch, cols), F32),
             vmem((layers, 3 * ch, 3 * ch), F32),
             vmem((layers, ns, 3 * ch // ns, 3 * ch), F32),
             vmem((layers, 3 * ch, 3 * ch), F32),
             vmem((layers * 9, ch, ch), F32),
-            dma((3,)), dma((3,)), dma((2,)), dma((2,)), dma((2,)), dma((2,)),
+            dma((3,)), dma((3,)), dma((4,)), dma((4,)), dma((2,)), dma((2,)),
             dma((nl,)), dma((nl,)),
             dma((nl,)), dma((phases, nl)), dma((nl,)), dma((phases, nl)),
             dma((phases, 4)), dma((phases, 4)),
@@ -616,6 +700,7 @@
         output_cotangent.reshape(ch, rows, 1, cols),
         conv_weights,
     )
+    states, starts, grads = publish(states.reshape(ch * rows, cols), starts.reshape(ch * rows, cols), grads)
     return (
         states.reshape(1, 1, ch, rows, cols),
         starts.reshape(1, 1, ch, rows, cols),

time: 148 us -> 126 us (0.85)
  Pallas kernels: 143 us -> 125 us
  local copies, waits for them, and re-layouts: 4.61 us -> 0 us
    pallas_call x1, Pallas kernels: 143 us -> 122 us  [per_device(): pl.pallas_call(functools.partial(kernel, nl, ns, rows, ch, cols, step_siz...]
    unnamed x7 -> x0, local copies, waits for them, and re-layouts: 4.61 us -> none
    pallas_call x0 -> x1, Pallas kernels: none -> 2.88 us  [publish(): pl.pallas_call(publish_body, grid=(steps,), out_shape=tuple((jax.ShapeDty...]
where the time goes in v3:
time: 126 us
  Pallas kernels  125 us (99%)
    pallas_call x1, Pallas kernels, per_device(): pl.pallas_call(functools.partial(kernel, nl, ns, rows, ch, cols, step_siz...  122 us
    pallas_call x1, Pallas kernels, publish(): pl.pallas_call(publish_body, grid=(steps,), out_shape=tuple((jax.ShapeDty...  2.88 us

profile of v3, /device:TPU:0, one launch (start us, length us, event | category | flops | bytes accessed | tf_op | source)
XLA Modules:
  0.0 126.0 jit_solution(5067136970605545081)
XLA Ops:
  0.6 122.4 %mgrit.1 = (f32[64,32,1,128]{3,2,1,0:T(1,128)}, f32[64,32,1,128]{3,2,1,0:T(1,128)}, f32[18,64,64]{2,1,0:T(8,128)}) custom-call(f32[64,32,1,128]{3,2,1,0:T(1,128)} %bitcast.7, f32[64,32,1,128]{3,2,1,0:T(1,128)} %bitcast.8, bf16[2,9,64,64]{3,2,1,0:T(8,128)(2,1)} %w_in.1), custom_call_target="tpu_custom_call" | custom-call | tf_op jit(solution)/shard_map/mgrit/pallas_call | solution.py:657
  123.1 2.9 %publish.1 = (f32[2048,128]{1,0:T(8,128)}, f32[2048,128]{1,0:T(8,128)}, f32[18,64,64]{2,1,0:T(8,128)}) custom-call(f32[2048,128]{1,0:T(8,128)} %bitcast.9, f32[2048,128]{1,0:T(8,128)} %bitcast.10, f32[18,64,64]{2,1,0:T(8,128)} %get-tuple-element.11.refs_2_), custom_call_target="tpu_custom_call" | custom-call | tf_op jit(solution)/shard_map/publish/pallas_call | solution.py:633

commit v4 on v3

--- a/solution.py
+++ b/solution.py
@@ -35,6 +35,7 @@
     groups = nl // GROUP
     spread_by = nl // 4
     my_row = lax.rem(me, spread_by) * 4 + lax.div(me, spread_by)
+    plane = lax.div(me, spread_by)
     has_up = space > 0
     has_down = space < ns - 1
 
@@ -167,9 +168,11 @@
     not_last = lane < cols - 1
 
     def shifted(v):
-        left = jnp.where(not_first, pltpu.roll(v, 1, 1), 0.0)
-        right = jnp.where(not_last, pltpu.roll(v, cols - 1, 1), 0.0)
-        return jnp.concatenate([left.astype(BF16), v.astype(BF16), right.astype(BF16)], axis=0)
+        v = v.astype(BF16)
+        nothing = jnp.zeros_like(v)
+        left = jnp.where(not_first, pltpu.roll(v, 1, 1), nothing)
+        right = jnp.where(not_last, pltpu.roll(v, cols - 1, 1), nothing)
+        return jnp.concatenate([left, v, right], axis=0)
 
     def inside(e):
         return jnp.logical_and(
@@ -204,9 +207,12 @@
                 if ph % ITERS:
                     entry = entry - sendq[ph - 1, r].astype(F32)
                 sendq[ph, r] = entry.astype(BF16)
-        for p in which:
-            for r in (2 * p - HALO, 2 * p + 1 - HALO):
-                pl.when(r != my_row)(lambda r=r: q_copy(ph, r, me).start())
+
+        def send():
+            for p in which:
+                for r in (2 * p - HALO, 2 * p + 1 - HALO):
+                    pl.when(r != my_row)(lambda r=r: q_copy(ph, r, me).start())
+        return send
 
     def wait_q_sent(ph):
         def one(i):
@@ -244,21 +250,26 @@
     def sweep(arrival, far, edge, first_value, first_weight, second_value, second_weight,
               finish, keeps=(None, None), spread=False, last=None):
         def begin(m):
-            block = lax.rem(lax.div(me, GROUP) + groups - m, groups)
-            places = [2 * block, 2 * block + 1]
-            if arrival is not None:
-                up, down = halo_copies(arrival, far)
-                for place in places:
-                    for row in (2 * place, 2 * place + 1):
-                        pl.when(row != my_row)(
-                            lambda row=row: x_copy(arrival, row, row).wait_recv())
-                    for at, copy in up:
-                        pl.when(jnp.logical_and(place == at, has_up))(copy.start)
-                    for at, copy in down:
-                        pl.when(jnp.logical_and(place == at, has_down))(copy.start)
+            if arrival is None:
+                convolve([first_own + 8 * m + k for k in range(8)],
+                         first_value, first_weight, y0, keeps[0])
+                return
+            places = []
+            for k in range(4):
+                block = lax.rem(lax.div(me, GROUP) + 2 * groups - 4 * m - k, groups)
+                places += [2 * block, 2 * block + 1]
+            up, down = halo_copies(arrival, far)
+            for place in places:
+                for row in (2 * place, 2 * place + 1):
+                    pl.when(row != my_row)(
+                        lambda row=row: x_copy(arrival, row, row).wait_recv())
+                for at, copy in up:
+                    pl.when(jnp.logical_and(place == at, has_up))(copy.start)
+                for at, copy in down:
+                    pl.when(jnp.logical_and(place == at, has_down))(copy.start)
             convolve([first_own + place for place in places],
                      first_value, first_weight, y0, keeps[0])
-        loop(0, own // 2, begin)
+        loop(0, own // 8, begin)
 
         def settle():
             if arrival is None:
@@ -294,23 +305,27 @@
             return
 
         def ring(n):
-            start = lax.div(lax.div(me, 2) * inner, own)
+            start = lax.rem(lax.div(lax.rem(me, spread_by), 2) + 2, spread_by // 2)
+            start = lax.div(lax.rem(4 * start + plane, own) * inner, own)
             return first_own + 2 + lax.rem(start + inner - 1 + n, inner)
 
         def second(which):
             convolve(which, second_value, second_weight, y1, keeps[1])
 
+        def both(done, which):
+            send = finish(done)
+            if send is not None:
+                send()
+            if which:
+                second(which)
+
         second([first_own + 1, pairs - first_own - 2])
         if inner:
-            second([ring(0), ring(1)])
-            second([ring(2), ring(3)])
-
-            def more(m):
-                finish([ring(2 * m - 3), ring(2 * m - 2)])
-                second([ring(2 * m), ring(2 * m + 1)])
-            loop(2, inner // 2, more)
-            finish([ring(inner - 3), ring(inner - 2)])
-            finish([ring(inner - 1), ring(0)])
+            q = [ring(n) for n in range(inner)]
+            second(q[:4])
+            for m in range(1, inner // 4):
+                both(q[max(4 * m - 5, 1):4 * m - 1], q[4 * m:4 * m + 4])
+            both(q[max(inner - 5, 1):] + q[:1], [])
         settle()
         rim()
         if spread:
@@ -319,8 +334,8 @@
             finish([1, pairs - 2])
         else:
             second([1, 2, pairs - 3, pairs - 2])
-        finish([2, 3])
-        finish([pairs - 4, pairs - 3])
+        both([2, 3], [])
+        both([pairs - 4, pairs - 3], [])
 
     def mixed(matrices, state):
         high = state.astype(BF16)
@@ -516,12 +531,11 @@
     wait_q_sent(3)
 
     quarter = 3 * ch // ns
+    many = 3 if (pairs - 2) % 3 == 0 else 2
 
     def gradient(layer, d, x):
         d[pl.ds(0, HALO)] = blank16
         d[pl.ds(HALO + rows, HALO)] = blank16
-
-        many = 3 if (pairs - 2) % 3 == 0 else 2
 
         def one(m, total):
             which = [1 + many * m + k for k in range(many)]
@@ -585,18 +599,23 @@
                 a1[e] = after
                 d0[e] = jnp.where(inside(e), scaled(t0[e], after), 0.0).astype(BF16)
 
-        def scale_two(m):
-            scale(1 + 2 * m)
-            scale(2 + 2 * m)
-        loop(0, (pairs - 2) // 2, scale_two)
+        def scale_some(m):
+            for k in range(many):
+                scale(1 + many * m + k)
+        loop(0, (pairs - 2) // many, scale_some)
         top, bottom = d0[HALO - 1], d0[HALO + rows]
         gradient(0, d0, x0)
         d0[HALO - 1] = top
         d0[HALO + rows] = bottom
 
+        wait_x_sent(3)
+        reduce_part(1)
+
         def second(m):
-            convolve([1 + 2 * m, 2 + 2 * m], lambda e: d0[e].astype(F32), wb.at[0], y1)
-        loop(0, (pairs - 2) // 2, second)
+            convolve([1 + many * m + k for k in range(many)],
+                     lambda e: d0[e].astype(F32), wb.at[0], y1)
+        loop(0, (pairs - 2) // many, second)
+        reduce_part(0)
 
         def end(m):
             for e in range(4):
@@ -607,9 +626,6 @@
     sweep(3, False, None, adjoint_first(3, a, True), wb.at[1], None, None, None, last=last_steps)
     for r in range(rows):
         pltpu.make_async_copy(a1.at[HALO + r], adj_out.at[:, r, 0], out_sem.at[1]).start()
-    wait_x_sent(3)
-    reduce_part(1)
-    reduce_part(0)
     collect(1)
     collect(0)
     grads = pltpu.make_async_copy(gout, grads_out, out_sem.at[2])
@@ -700,7 +716,9 @@
         output_cotangent.reshape(ch, rows, 1, cols),
         conv_weights,
     )
-    states, starts, grads = publish(states.reshape(ch * rows, cols), starts.reshape(ch * rows, cols), grads)
+    states, starts, grads = publish(
+        states.reshape(ch * rows, cols), starts.reshape(ch * rows, cols),
+        grads.reshape(layers * 9 * ch, ch))
     return (
         states.reshape(1, 1, ch, rows, cols),
         starts.reshape(1, 1, ch, rows, cols),

time: 126 us -> 120 us (0.952)
  Pallas kernels: 125 us -> 119 us
    pallas_call x1, Pallas kernels: 122 us -> 116 us  [per_device(): pl.pallas_call(functools.partial(kernel, nl, ns, rows, ch, cols, step_siz...]
where the time goes in v4:
time: 120 us
  Pallas kernels  119 us (99%)
    pallas_call x1, Pallas kernels, per_device(): pl.pallas_call(functools.partial(kernel, nl, ns, rows, ch, cols, step_siz...  116 us
    pallas_call x1, Pallas kernels, publish(): pl.pallas_call(publish_body, grid=(steps,), out_shape=tuple((jax.ShapeDty...  2.88 us

profile of v4, /device:TPU:0, one launch (start us, length us, event | category | flops | bytes accessed | tf_op | source)
XLA Modules:
  0.0 119.9 jit_solution(6990198125179353174)
XLA Ops:
  0.6 116.3 %mgrit.1 = (f32[64,32,1,128]{3,2,1,0:T(1,128)}, f32[64,32,1,128]{3,2,1,0:T(1,128)}, f32[18,64,64]{2,1,0:T(8,128)}) custom-call(f32[64,32,1,128]{3,2,1,0:T(1,128)} %bitcast.8, f32[64,32,1,128]{3,2,1,0:T(1,128)} %bitcast.9, bf16[2,9,64,64]{3,2,1,0:T(8,128)(2,1)} %w_in.1), custom_call_target="tpu_custom_call" | custom-call | tf_op jit(solution)/shard_map/mgrit/pallas_call | solution.py:673
  117.0 2.9 %publish.1 = (f32[2048,128]{1,0:T(8,128)}, f32[2048,128]{1,0:T(8,128)}, f32[1152,64]{1,0:T(8,128)}) custom-call(f32[2048,128]{1,0:T(8,128)} %bitcast.10, f32[2048,128]{1,0:T(8,128)} %bitcast.11, f32[1152,64]{1,0:T(8,128)} %bitcast.12), custom_call_target="tpu_custom_call" | custom-call | tf_op jit(solution)/shard_map/publish/pallas_call | solution.py:649

commit v5 on v4

--- a/solution.py
+++ b/solution.py
@@ -405,8 +405,8 @@
 
         def spread_group(n):
             targets = []
-            for t in range(2):
-                g = lax.rem(lax.div(my_row, GROUP) + 2 * n + t, groups)
+            for t in range(4):
+                g = lax.rem(lax.div(my_row, GROUP) + 4 * n + t, groups)
                 if reverse:
                     g = groups - 1 - g
                 start = ys[GROUP * g + GROUP - 1]
@@ -420,7 +420,7 @@
                     targets.append(j)
             for j in targets:
                 pl.when(j != me)(lambda j=j: x_copy(ph, j, my_row).start())
-        loop(0, groups // 2, spread_group)
+        loop(0, groups // 4, spread_group)
         recvx[ph, HALO + my_row] = sendx[ph, me]
 
     c_edge = edge_copies(c, 2, ch_send, ch_recv)
@@ -531,7 +531,7 @@
     wait_q_sent(3)
 
     quarter = 3 * ch // ns
-    many = 3 if (pairs - 2) % 3 == 0 else 2
+    many = 6 if (pairs - 2) % 6 == 0 else 2
 
     def gradient(layer, d, x):
         d[pl.ds(0, HALO)] = blank16

time: 120 us -> 120 us (level)
  no operation moved by 1% of the time
where the time goes in v5:
time: 120 us; the launch traced here: 119 us
  Pallas kernels  118 us (98%)
    pallas_call x1, Pallas kernels, per_device(): pl.pallas_call(functools.partial(kernel, nl, ns, rows, ch, cols, step_siz...  115 us
    pallas_call x1, Pallas kernels, publish(): pl.pallas_call(publish_body, grid=(steps,), out_shape=tuple((jax.ShapeDty...  2.88 us

profile of v5, /device:TPU:0, one launch (start us, length us, event | category | flops | bytes accessed | tf_op | source)
XLA Modules:
  0.0 118.9 jit_solution(5206898894070740405)
XLA Ops:
  0.6 115.4 %mgrit.1 = (f32[64,32,1,128]{3,2,1,0:T(1,128)}, f32[64,32,1,128]{3,2,1,0:T(1,128)}, f32[18,64,64]{2,1,0:T(8,128)}) custom-call(f32[64,32,1,128]{3,2,1,0:T(1,128)} %bitcast.8, f32[64,32,1,128]{3,2,1,0:T(1,128)} %bitcast.9, bf16[2,9,64,64]{3,2,1,0:T(8,128)(2,1)} %w_in.1), custom_call_target="tpu_custom_call" | custom-call | tf_op jit(solution)/shard_map/mgrit/pallas_call | solution.py:673
  116.0 2.9 %publish.1 = (f32[2048,128]{1,0:T(8,128)}, f32[2048,128]{1,0:T(8,128)}, f32[1152,64]{1,0:T(8,128)}) custom-call(f32[2048,128]{1,0:T(8,128)} %bitcast.10, f32[2048,128]{1,0:T(8,128)} %bitcast.11, f32[1152,64]{1,0:T(8,128)} %bitcast.12), custom_call_target="tpu_custom_call" | custom-call | tf_op jit(solution)/shard_map/publish/pallas_call | solution.py:649
